TPU v7x, 32 devices: a whole 2x2x4 slice. The times are simulated.
32 devices in a mesh: dp: 2 (over y), blk: 16 (over z, x, core).
Axes of the slice: x: 2, y: 2, z: 4, core: 2. Of those that a mesh axis runs over, the one named last changes fastest.
Arguments:
- tokens: bfloat16 [2, 16384, 768], P(None, ('dp', 'blk')), may hold values from -6 to 6
- memory: bfloat16 [2, 8, 20, 768], P(None, 'dp'), may hold values from -6 to 6
- chain_lengths: int32 [2, 2, 4], P(None, 'dp'), may hold values from 1 to 7, 16 in all within a row
- last_fill: int32 [2, 2, 4], P(None, 'dp'), may hold values from 1 to 512
- query_proj: bfloat16 [768, 768], replicated, may hold values from -0.21875 to 0.21875
- query_bias: bfloat16 [768], replicated, may hold values from -1.75 to 1.75
- key_proj: bfloat16 [768, 768], replicated, may hold values from -0.21875 to 0.21875
- value_proj: bfloat16 [768, 768], replicated, may hold values from -0.21875 to 0.21875
- value_bias: bfloat16 [768], replicated, may hold values from -1.75 to 1.75
- output_proj: bfloat16 [768, 768], replicated, may hold values from -3.5 to 3.5
- output_bias: bfloat16 [768], replicated, may hold values from -1.75 to 1.75
- attn_gain: bfloat16 [768], replicated, may hold values from 0.5 to 1.5
- attn_shift: bfloat16 [768], replicated, may hold values from -1.75 to 1.75
- inner_proj: bfloat16 [768, 3072], replicated, may hold values from -0.21875 to 0.21875
- inner_bias: bfloat16 [3072], replicated, may hold values from -1.75 to 1.75
- outer_proj: bfloat16 [3072, 768], replicated, may hold values from -0.109375 to 0.109375
- outer_bias: bfloat16 [768], replicated, may hold values from -1.75 to 1.75
- final_gain: bfloat16 [768], replicated, may hold values from 0.5 to 1.5
- final_shift: bfloat16 [768], replicated, may hold values from -1.75 to 1.75
- token_cotangent: bfloat16 [2, 16384, 768], P(None, ('dp', 'blk')), may hold values from -6 to 6
- memory_cotangent: bfloat16 [2, 8, 20, 768], P(None, 'dp'), may hold values from -6 to 6
Outputs:
- layer_output: bfloat16 [2, 16384, 768], P(None, ('dp', 'blk'))
- memory_output: bfloat16 [2, 8, 20, 768], P(None, 'dp')
- token_grad: bfloat16 [2, 16384, 768], P(None, ('dp', 'blk'))
- memory_grad: bfloat16 [2, 8, 20, 768], P(None, 'dp')
- grad_query_proj: float32 [768, 768], replicated
- grad_query_bias: float32 [768], replicated
- grad_key_proj: float32 [768, 768], replicated
- grad_value_proj: float32 [768, 768], replicated
- grad_value_bias: float32 [768], replicated
- grad_output_proj: float32 [768, 768], replicated
- grad_output_bias: float32 [768], replicated
- grad_attn_gain: float32 [768], replicated
- grad_attn_shift: float32 [768], replicated
- grad_inner_proj: float32 [768, 3072], replicated
- grad_inner_bias: float32 [3072], replicated
- grad_outer_proj: float32 [3072, 768], replicated
- grad_outer_bias: float32 [768], replicated
- grad_final_gain: float32 [768], replicated
- grad_final_shift: float32 [768], replicated
Inputs may be any that keep to these rules, and one draw needn't show every extreme that they name: `chain_lengths`: the lengths of each group's 4 chains add up to 16, and the longest chain of each group has 7 segments. The tokens of a chain's last segment after last_fill are padding.
All inputs are finite; a program needn't handle non-finite values.
Results may differ from a plain program's by a relative error of at most 0.02.
Values may be sent and summed in bfloat16 or wider, within the bound.
No kernel may reach another device: no remote copies, remote signals or barrier semaphores. Data moves between devices by JAX's collectives and lax.ppermute only.
A program may use at most 384 MiB of HBM per device.

v0:
```python
import functools

import jax
import jax.numpy as jnp
from jax import lax
from jax.experimental import pallas as pl
from jax.experimental.pallas import tpu as pltpu
from jax.sharding import PartitionSpec as P

H = 12
HD = 64
QUAD = 256
NQUAD = 3
PAIR = 128
MEMP = 32
SEG = 512
LONG = 7
NBLK = LONG + 1
CAP = NBLK * SEG
OWN = SEG + MEMP
STAT = 24
BACK_COST = 10_000_000_000
LATE_ROWS = 256
NPIECE = 14
ROWS = 272
COLS = 1024
NEG = -1e30
SHIFT_FREE = 60.0
EPS = 1e-05
F32 = jnp.float32
BF16 = jnp.bfloat16
VMEM_LIMIT = 60 * 2**20
LAST = (((1,), (1,)), ((), ()))

M_LEN, M_ROWS, M_BLOCKS, M_SPOT, M_USED, M_MEM, M_CHAIN, M_START, M_PIECE = range(9)


def plane_moves(shift_of):
    pairs = []
    for plane in range(4):
        for place in range(4):
            target = plane + shift_of(place >> 1)
            if 0 <= target < 4:
                pairs.append((4 * plane + place, 4 * target + place))
    return pairs


UP = plane_moves(lambda side: 1)
DOWN = plane_moves(lambda side: -1)
OUTWARD = plane_moves(lambda side: 1 if side else -1)
SIDE = [(i, i ^ 2) for i in range(16)]
CORE = [(i, i ^ 1) for i in range(16)]


def move(value, pairs):
    return lax.ppermute(value, "blk", pairs)


def gather_near(value, others):
    side = (lax.axis_index("blk") >> 1) & 1
    below, above, beside = move(value, UP), move(value, DOWN), move(value, SIDE)
    below, others = lax.optimization_barrier((below, others))
    far = move(jnp.where(side == 1, below, above), OUTWARD)
    moved = [move(beside, UP), move(beside, DOWN), move(far, SIDE)]
    here = [value, beside, below, above] + moved
    return here + [move(part, CORE) for part in here], others


def gather_all(value):
    return [lax.all_gather(value, "blk")]


def piece_of(own, other):
    plane = (other >> 2) - (own >> 2)
    same_side = ((other >> 1) & 1) == ((own >> 1) & 1)
    on_side = jnp.where(plane == 0, 0, jnp.where(plane < 0, 2, 3))
    off_side = jnp.where(plane == 0, 1, jnp.where(plane == -1, 4, jnp.where(plane == 1, 5, 6)))
    index = jnp.where(same_side, on_side, off_side)
    return index + jnp.where((other & 1) == (own & 1), 0, LONG)


def meta_body(own_ref, lengths, fills, meta, *, batches, chains, mem_rows):
    own = own_ref[0]
    for b in range(batches):
        end = jnp.int32(0)
        length, start, fill, chain = (jnp.int32(0) for _ in range(4))
        for c in range(chains):
            begin = end
            end = end + lengths[b, c]
            inside = (begin <= own) & (own < end)
            length = jnp.where(inside, lengths[b, c], length)
            start = jnp.where(inside, begin, start)
            fill = jnp.where(inside, fills[b, c], fill)
            chain = jnp.where(inside, c, chain)
        rows = MEMP + SEG * (length - 1) + fill
        spot = own - start
        meta[b, M_LEN] = length
        meta[b, M_ROWS] = rows
        meta[b, M_BLOCKS] = (rows + SEG - 1) // SEG
        meta[b, M_SPOT] = spot
        meta[b, M_USED] = jnp.where(spot == length - 1, fill, SEG)
        meta[b, M_MEM] = jnp.int32(mem_rows)
        meta[b, M_CHAIN] = chain
        meta[b, M_START] = start
        for place in range(8):
            meta[b, M_PIECE + place] = piece_of(own, start + place)


def metas_of(own, lengths, fills, mem_rows):
    smem = pl.BlockSpec(memory_space=pltpu.SMEM)
    body = functools.partial(
        meta_body, batches=lengths.shape[0], chains=lengths.shape[1], mem_rows=mem_rows
    )
    return pl.pallas_call(
        body,
        in_specs=[smem] * 3,
        out_specs=smem,
        out_shape=jax.ShapeDtypeStruct((lengths.shape[0], 16), jnp.int32),
        name="find_chain",
    )(own.reshape(1), lengths, fills)


def load_chain(meta, pieces, view_from, view_to, sems):
    length = meta[M_LEN]
    for spot in range(LONG):
        def start(source):
            pltpu.make_async_copy(view_from(source), view_to(spot), sems.at[spot]).start()

        @pl.when(spot < length)
        def _():
            if len(pieces) == 1:
                start(pieces[0].at[meta[M_START] + spot])
                return
            for index in range(len(pieces)):
                @pl.when(meta[M_PIECE + spot] == index)
                def _():
                    start(pieces[index])


def wait_chain(meta, pieces, view_from, view_to, sems):
    length = meta[M_LEN]
    source = pieces[0].at[0] if len(pieces) == 1 else pieces[0]
    for spot in range(LONG):
        @pl.when(spot < length)
        def _():
            pltpu.make_async_copy(view_from(source), view_to(spot), sems.at[spot]).wait()


def key_bias(meta):
    column = lax.broadcasted_iota(jnp.int32, (8, CAP), 1)
    dead = (column >= meta[M_ROWS]) | ((column >= meta[M_MEM]) & (column < MEMP))
    return jnp.where(dead, NEG, 0.0).astype(F32)


def by_chunks(blocks, run):
    def four(index, carry):
        run(index * 4, 4)
        return carry

    lax.fori_loop(0, blocks // 4, four, 0)
    for count in (1, 2, 3):
        @pl.when(blocks % 4 == count)
        def _():
            run((blocks // 4) * 4, count)


def span_of(first, count):
    return pl.ds(pl.multiple_of(first * SEG, SEG), count * SEG)


def forward_body(meta, *refs):
    pieces, refs = refs[:-16], refs[-16:]
    mem, wq, wk, wv, bq, bv, out, lse, kc, vc, qc, rows, qown, extended, acc, sems = refs
    quad = pl.program_id(0)
    width = rows.shape[1]
    length, blocks = meta[M_LEN], meta[M_BLOCKS]
    here = lambda source: source
    there = lambda spot: rows.at[pl.ds(MEMP + SEG * spot, SEG)]

    @pl.when(quad == 0)
    def _():
        load_chain(meta, pieces, here, there, sems)
        rows[0:MEMP, :] = mem[meta[M_CHAIN]]
        lse[...] = jnp.zeros_like(lse)

        @pl.when(blocks > length)
        def _():
            place = pl.multiple_of(MEMP + SEG * length, MEMP)
            rows[pl.ds(place, SEG - MEMP), :] = jnp.zeros((SEG - MEMP, width), BF16)

        wait_chain(meta, pieces, here, there, sems)

    def longest(values):
        halves = [
            jnp.max(jnp.sum(jnp.square(values[:, p : p + PAIR]), axis=1, keepdims=True))
            for p in range(0, QUAD, PAIR)
        ]
        return jnp.maximum(*halves)

    def project(start, count):
        span = pl.ds(pl.multiple_of(start, MEMP), count)
        part = rows[span, :]
        row = start + lax.broadcasted_iota(jnp.int32, (count, QUAD), 0)
        alive = (row < meta[M_ROWS]) & ((row < meta[M_MEM]) | (row >= MEMP))
        lower = (lax.broadcasted_iota(jnp.int32, (count, QUAD), 1) % PAIR) < HD
        key = jnp.dot(part, wk[...], preferred_element_type=F32)
        kc[span, :] = key.astype(BF16)
        value = jnp.dot(part, wv[...], preferred_element_type=F32) + bv[...].astype(F32)
        vc[span, :] = value.astype(BF16)
        value = jnp.where(alive, value, 0.0)
        one = jnp.where(alive, 1.0, 0.0)
        extended[0, span, :] = jnp.where(lower, value, one).astype(BF16)
        extended[1, span, :] = jnp.where(lower, one, value).astype(BF16)
        query = jnp.dot(part, wq[...], preferred_element_type=F32) + bq[...].astype(F32)
        query = query.astype(BF16) * jnp.asarray(HD**-0.5, BF16)
        qc[span, :] = query
        return longest(key)

    def project_block(block, top):
        return jnp.maximum(top, project(block * SEG, SEG))

    key_top = lax.fori_loop(0, blocks, project_block, jnp.float32(0.0))

    @pl.when(blocks == length)
    def _():
        project(length * SEG, MEMP)

    place = pl.multiple_of(MEMP + SEG * meta[M_SPOT], MEMP)
    qown[0:SEG, :] = qc[pl.ds(place, SEG), :]
    qown[SEG:OWN, :] = qc[0:MEMP, :]
    near = longest(qown[...].astype(F32)) * key_top <= SHIFT_FREE**2

    def pair(index, carry):
        cols = pl.ds(pl.multiple_of(index * PAIR, PAIR), PAIR)
        lane = lax.broadcasted_iota(jnp.int32, (OWN, PAIR), 1)
        halves = (0, 1)
        mine = [(lane // HD) == half for half in halves]
        numbers = [lane == quad * 4 + index * 2 + half for half in halves]
        both = qown[:, cols]
        queries = [jnp.where(mine[half], both, jnp.zeros_like(both)) for half in halves]
        acc[...] = jnp.zeros_like(acc)

        def score(half, span):
            return lax.dot_general(queries[half], kc[span, cols], LAST, preferred_element_type=F32)

        def gather(half, span, terms):
            values = extended[half, span, cols]
            return jnp.dot(terms.astype(BF16), values, preferred_element_type=F32)

        @pl.when(near)
        def _():
            def run(first, count):
                span = span_of(first, count)
                for half in halves:
                    acc[half] += gather(half, span, jnp.exp(score(half, span)))

            by_chunks(blocks, run)

        @pl.when(jnp.logical_not(near))
        def _():
            for half in halves:
                def run(block, top):
                    span = span_of(block, 1)
                    column = block * SEG + lax.broadcasted_iota(jnp.int32, (OWN, SEG), 1)
                    dead = (column >= meta[M_ROWS]) | ((column >= meta[M_MEM]) & (column < MEMP))
                    scores = jnp.where(dead, NEG, score(half, span))
                    new = jnp.maximum(top, jnp.max(scores, axis=1, keepdims=True))
                    terms = gather(half, span, jnp.exp(scores - new))
                    acc[half] = acc[half] * jnp.exp(top - new) + terms
                    return new

                top = lax.fori_loop(0, blocks, run, jnp.full((OWN, 1), NEG, F32))
                lse[...] = jnp.where(numbers[half], top, lse[...])

        sums = [acc[half] for half in halves]
        value = jnp.where(mine[0], sums[0], sums[1])
        total = pltpu.roll(jnp.where(mine[0], sums[1], sums[0]), HD, 1)
        out[:, cols] = value * (1.0 / total)
        turned_total = pltpu.roll(total, HD, 1)
        for half in halves:
            spread = jnp.where(mine[half], total, turned_total)
            lse[...] += jnp.where(numbers[half], jnp.log(spread), 0.0)
        return carry

    lax.fori_loop(0, 2, pair, 0)


def attend_forward(meta, pieces, mem, weights):
    wq, bq, wk, wv, bv = weights
    width = wq.shape[0]
    whole = lambda shape: pl.BlockSpec(shape, lambda quad, meta: (0,) * len(shape))
    column = lambda count: pl.BlockSpec((count, QUAD), lambda quad, meta: (0, quad))
    return pl.pallas_call(
        forward_body,
        grid_spec=pltpu.PrefetchScalarGridSpec(
            num_scalar_prefetch=1,
            grid=(NQUAD,),
            in_specs=[pl.BlockSpec(memory_space=pl.ANY)] * len(pieces)
            + [whole((mem.shape[0], MEMP, width))]
            + [column(width)] * 3
            + [column(1)] * 2,
            out_specs=[column(OWN), whole((OWN, PAIR))] + [column(CAP)] * 3,
            scratch_shapes=[
                pltpu.VMEM((CAP, width), BF16),
                pltpu.VMEM((OWN, QUAD), BF16),
                pltpu.VMEM((2, CAP, QUAD), BF16),
                pltpu.VMEM((2, OWN, PAIR), F32),
                pltpu.SemaphoreType.DMA((LONG,)),
            ],
        ),
        out_shape=[
            jax.ShapeDtypeStruct((OWN, width), F32),
            jax.ShapeDtypeStruct((OWN, PAIR), F32),
        ]
        + [jax.ShapeDtypeStruct((CAP, width), BF16)] * 3,
        compiler_params=pltpu.CompilerParams(vmem_limit_bytes=VMEM_LIMIT),
        cost_estimate=pl.CostEstimate(
            flops=40_000_000_000, bytes_accessed=30_000_000, transcendentals=23_000_000
        ),
        name="attend_forward",
    )(meta, *pieces, mem, wq, wk, wv, bq.reshape(1, -1), bv.reshape(1, -1))


def backward_body(start, count, meta, *refs):
    pieces, refs = refs[:-22], refs[-22:]
    (
        kc, vc, qc, mem_grad, mem_stats, own_stats,
        dq, dk, dv,
        doc, stats, chain_stats, qown, kown, vown, down, bias, qacc, kacc, vacc, sems, stat_sems,
    ) = refs
    step = pl.program_id(0)
    quad = start + step
    length = meta[M_LEN]

    @pl.when(step == 0)
    def _():
        rows_from = lambda index: lambda ref: ref.at[0:SEG, pl.ds((start + index) * QUAD, QUAD)]
        rows_to = lambda index: lambda spot: doc.at[index, pl.ds(MEMP + SEG * spot, SEG)]
        stat_from = lambda ref: ref.at[SEG : SEG + 2 * STAT, 0:SEG]
        stat_to = lambda spot: stats.at[spot]
        load_chain(meta, pieces, stat_from, stat_to, stat_sems)
        for index in range(count):
            load_chain(meta, pieces, rows_from(index), rows_to(index), sems.at[index])
        bias[...] = key_bias(meta)
        for index in range(count):
            doc[index, 0:MEMP, :] = mem_grad[:, (start + index) * QUAD : (start + index + 1) * QUAD]

            @pl.when(meta[M_BLOCKS] > length)
            def _():
                place = pl.multiple_of(MEMP + SEG * length, MEMP)
                doc[index, pl.ds(place, SEG - MEMP), :] = jnp.zeros((SEG - MEMP, QUAD), BF16)

        wait_chain(meta, pieces, stat_from, stat_to, stat_sems)
        for spot in range(NBLK):
            span = slice(SEG * spot, SEG * (spot + 1))
            if spot == LONG:
                chain_stats[:, span] = jnp.zeros((STAT, SEG), F32)
                continue

            @pl.when(spot < length)
            def _():
                pair = stats[spot].astype(F32)
                chain_stats[:, span] = pair[0:STAT] + pair[STAT : 2 * STAT]

            @pl.when(spot >= length)
            def _():
                chain_stats[:, span] = jnp.zeros((STAT, SEG), F32)

        moved = pltpu.roll(chain_stats[...], MEMP, 1)
        column = lax.broadcasted_iota(jnp.int32, (STAT, CAP), 1)
        entry = lax.broadcasted_iota(jnp.int32, (STAT, CAP), 0)
        beyond = jnp.where(entry < H, -NEG, 0.0)
        chain_stats[...] = jnp.where(column < MEMP + SEG * length, moved, beyond)
        lane = lax.broadcasted_iota(jnp.int32, (STAT, PAIR), 1)
        at_front = pltpu.roll(mem_stats[...], MEMP, 1)
        chain_stats[:, 0:PAIR] = jnp.where(lane < MEMP, at_front, chain_stats[:, 0:PAIR])
        for index in range(count):
            wait_chain(meta, pieces, rows_from(index), rows_to(index), sems.at[index])

    place = pl.multiple_of(MEMP + SEG * meta[M_SPOT], MEMP)
    for own, chain in ((qown, qc), (kown, kc), (vown, vc), (down, doc.at[step])):
        own[0:SEG, :] = chain[pl.ds(place, SEG), :]
        own[SEG:OWN, :] = chain[0:MEMP, :]

    def head(index, carry):
        cols = pl.ds(pl.multiple_of((index // 2) * PAIR, PAIR), PAIR)
        number = quad * 4 + index
        lane = lax.broadcasted_iota(jnp.int32, (OWN, PAIR), 1)
        mine = (lane // HD) == (index % 2)
        masked = lambda ref: jnp.where(mine, ref[:, cols], jnp.zeros((OWN, PAIR), BF16))
        query, key, value, grad = masked(qown), masked(kown), masked(vown), masked(down)
        pick = lambda at: jnp.sum(jnp.where(lane == at, own_stats[...], 0.0), axis=1, keepdims=True)
        log_total, delta = pick(number), pick(H + number)
        for acc in (qacc, kacc, vacc):
            acc[...] = jnp.zeros_like(acc)

        def run(first, size):
            span = span_of(first, size)
            keys, values = kc[span, cols], vc[span, cols]
            scores = lax.dot_general(query, keys, LAST, preferred_element_type=F32)
            weights = jnp.exp(scores + bias[0:1, span] - log_total)
            weight_grad = lax.dot_general(grad, values, LAST, preferred_element_type=F32)
            score_grad = (weights * (weight_grad - delta)).astype(BF16)
            qacc[...] += jnp.dot(score_grad, keys, preferred_element_type=F32)

            queries, grads = qc[span, cols], doc[step, span, cols]
            scores = lax.dot_general(key, queries, LAST, preferred_element_type=F32)
            weights = jnp.exp(scores - chain_stats[pl.ds(number, 1), span])
            weight_grad = lax.dot_general(value, grads, LAST, preferred_element_type=F32)
            score_grad = (
                weights * (weight_grad - chain_stats[pl.ds(H + number, 1), span])
            ).astype(BF16)
            vacc[...] += jnp.dot(weights.astype(BF16), grads, preferred_element_type=F32)
            kacc[...] += jnp.dot(score_grad, queries, preferred_element_type=F32)

        by_chunks(meta[M_BLOCKS], run)
        row = lax.broadcasted_iota(jnp.int32, (OWN, PAIR), 0)
        alive = (row < meta[M_USED]) | ((row >= SEG) & (row < SEG + meta[M_MEM]))
        query_sum = qacc[...] * (HD**-0.5)
        key_sum = jnp.where(alive, kacc[...], 0.0)
        value_sum = jnp.where(alive, vacc[...], 0.0)
        for ref, sums in ((dq, query_sum), (dk, key_sum), (dv, value_sum)):
            ref[:, cols] = jnp.where(mine, sums.astype(BF16), ref[:, cols])
        return carry

    lax.fori_loop(0, 4, head, 0)


def attend_backward(meta, pieces, chain, mem_grad, mem_stats, own_stats, start, count):
    width = mem_grad.shape[1]
    whole = lambda shape: pl.BlockSpec(shape, lambda quad, meta: (0,) * len(shape))
    chain_column = pl.BlockSpec((CAP, QUAD), lambda step, meta: (0, start + step))
    own_column = pl.BlockSpec((OWN, QUAD), lambda step, meta: (0, step))
    return pl.pallas_call(
        functools.partial(backward_body, start, count),
        grid_spec=pltpu.PrefetchScalarGridSpec(
            num_scalar_prefetch=1,
            grid=(count,),
            in_specs=[pl.BlockSpec(memory_space=pl.ANY)] * len(pieces)
            + [chain_column] * 3
            + [whole((MEMP, width)), whole((STAT, PAIR)), whole((OWN, PAIR))],
            out_specs=[own_column] * 3,
            scratch_shapes=[
                pltpu.VMEM((count, CAP, QUAD), BF16),
                pltpu.VMEM((LONG, 2 * STAT, SEG), BF16),
                pltpu.VMEM((STAT, CAP), F32),
            ]
            + [pltpu.VMEM((OWN, QUAD), BF16)] * 4
            + [
                pltpu.VMEM((8, CAP), F32),
                pltpu.VMEM((OWN, PAIR), F32),
                pltpu.VMEM((OWN, PAIR), F32),
                pltpu.VMEM((OWN, PAIR), F32),
                pltpu.SemaphoreType.DMA((count, LONG)),
                pltpu.SemaphoreType.DMA((LONG,)),
            ],
        ),
        out_shape=[jax.ShapeDtypeStruct((OWN, count * QUAD), BF16)] * 3,
        compiler_params=pltpu.CompilerParams(vmem_limit_bytes=VMEM_LIMIT),
        cost_estimate=pl.CostEstimate(
            flops=BACK_COST, bytes_accessed=1_000_000, transcendentals=0
        ),
        name="attend_backward",
    )(meta, *pieces, *chain, mem_grad, mem_stats, own_stats)


def norm_stats(values):
    centered = values - jnp.mean(values, axis=-1, keepdims=True)
    scale = lax.rsqrt(jnp.mean(centered * centered, axis=-1, keepdims=True) + EPS)
    return centered * scale, scale


def norm_back(normed, scale, upstream):
    mean = jnp.mean(upstream, axis=-1, keepdims=True)
    along = jnp.mean(upstream * normed, axis=-1, keepdims=True)
    return scale * (upstream - mean - normed * along)


def turned(left, right):
    return lax.dot_general(left, right, LAST, preferred_element_type=F32)


def crossed(left, right):
    return lax.dot_general(left, right, (((0,), (0,)), ((), ())), preferred_element_type=F32)


def middle_body(
    meta, attended, lse, tokens, memory, token_cot, memory_cot,
    wo, bo, gain1, shift1, bi, b2, gain2, shift2, wi_from, w2_from,
    final, final_mem, payload, mem_grad, mem_stats, own_stats, res_grad, rows,
    attended_low, branch_out, first_low, inner_out, active, outer_out, sums, inner_sum,
    wi, w2, first, norm1, scale1, total, second_grad, outer_grad, slope, cots, weight_sems,
):
    width, inner_width = wi.shape
    wi_copy = pltpu.make_async_copy(wi_from, wi, weight_sems.at[0])
    w2_copy = pltpu.make_async_copy(w2_from, w2, weight_sems.at[1])
    wi_copy.start()
    w2_copy.start()
    chain = meta[M_CHAIN]
    lead = jnp.where(meta[M_SPOT] == 0, 1.0, 0.0)
    rows[0:SEG, :] = tokens[...]
    rows[SEG:OWN, :] = memory[chain]
    cots[0:SEG, :] = token_cot[...]
    cots[SEG:OWN, :] = memory_cot[chain]
    attended_low[...] = attended[...].astype(BF16)
    total[...] = jnp.dot(attended_low[...], wo[...], preferred_element_type=F32)
    sums[...] = jnp.zeros_like(sums)
    inner_sum[...] = jnp.zeros_like(inner_sum)
    vector = lambda ref: ref[...].astype(F32)

    def by_rows(run):
        def step(index, carry):
            start = pl.multiple_of(index * ROWS, ROWS)
            row = start + lax.broadcasted_iota(jnp.int32, (ROWS, 1), 0)
            live = (row < meta[M_USED]) | ((row >= SEG) & (row < SEG + meta[M_MEM]))
            counted = jnp.where(row < SEG, 1.0, lead)
            run(pl.ds(start, ROWS), live, counted)
            return carry

        lax.fori_loop(0, OWN // ROWS, step, 0)

    def by_columns(run):
        def step(index, carry):
            run(pl.ds(pl.multiple_of(index * COLS, COLS), COLS))
            return carry

        lax.fori_loop(0, inner_width // COLS, step, 0)

    def add(place, value):
        sums[place : place + 1, :] += jnp.sum(value, axis=0, keepdims=True)

    def first_part(span, live, counted):
        value = rows[span, :].astype(F32) + total[span, :] + vector(bo)
        normed, scale = norm_stats(value)
        norm1[span, :] = normed
        scale1[span, :] = jnp.broadcast_to(scale, (ROWS, PAIR))
        value = normed * vector(gain1) + vector(shift1)
        first[span, :] = value
        first_low[span, :] = value.astype(BF16)

    by_rows(first_part)
    wi_copy.wait()
    w2_copy.wait()
    total[...] = jnp.zeros_like(total)

    def inner_part(cols):
        inner = jnp.dot(first_low[...], wi[:, cols], preferred_element_type=F32)
        inner = inner + bi[:, cols].astype(F32)
        cdf = 0.5 * (1.0 + lax.erf(inner * (2.0**-0.5)))
        density = jnp.exp(-0.5 * inner * inner) * 0.3989422804014327
        slope[:, cols] = cdf + inner * density
        low = (inner * cdf).astype(BF16)
        active[:, cols] = low
        total[...] += jnp.dot(low, w2[cols, :], preferred_element_type=F32)

    by_columns(inner_part)

    def final_part(span, live, counted):
        normed, scale = norm_stats(first[span, :] + total[span, :] + vector(b2))
        value = jnp.where(live, normed * vector(gain2) + vector(shift2), 0.0)
        rows_low = value.astype(BF16)
        outer_out[span, :] = rows_low
        cot = cots[span, :].astype(F32)
        cot = jnp.where(live, cot, 0.0)
        weighted = cot * counted
        add(4, weighted * normed)
        add(5, weighted)
        grad = norm_back(normed, scale, cot * vector(gain2))
        second_grad[span, :] = grad
        outer_grad[span, :] = grad.astype(BF16)
        add(3, grad.astype(BF16).astype(F32) * counted)

    by_rows(final_part)
    final[...] = outer_out[0:SEG, :]
    final_mem[...] = outer_out[SEG:OWN, :]
    outer_out[0:SEG, :] = outer_grad[0:SEG, :]
    outer_out[SEG:OWN, :] = outer_grad[SEG:OWN, :] * lead.astype(BF16)
    total[...] = jnp.zeros_like(total)

    def inner_back(cols):
        grad = (turned(outer_grad[...], w2[cols, :]) * slope[:, cols]).astype(BF16)
        total[...] += turned(grad, wi[:, cols])
        tail = grad[SEG:OWN] * lead.astype(BF16)
        inner_out[0:SEG, cols] = grad[0:SEG]
        inner_out[SEG:OWN, cols] = tail
        inner_sum[:, cols] = jnp.sum(grad[0:SEG].astype(F32), axis=0, keepdims=True) + jnp.sum(
            tail.astype(F32), axis=0, keepdims=True
        )

    by_columns(inner_back)

    def last_part(span, live, counted):
        grad = second_grad[span, :] + total[span, :]
        normed = norm1[span, :]
        weighted = grad * counted
        add(1, weighted * normed)
        add(2, weighted)
        grad = norm_back(normed, scale1[span, 0:1], grad * vector(gain1))
        res_grad[span, :] = grad
        low = grad.astype(BF16)
        outer_grad[span, :] = low
        low = (low.astype(F32) * counted).astype(BF16)
        branch_out[span, :] = low
        add(0, low.astype(F32))

    by_rows(last_part)
    total[...] = turned(outer_grad[...], wo[...])
    feature = lax.broadcasted_iota(jnp.int32, (width, PAIR), 0)
    lane = lax.broadcasted_iota(jnp.int32, (width, PAIR), 1)
    head_of = jnp.where(feature // HD == lane - H, 1.0, 0.0).astype(BF16)

    def delta_part(span, live, counted):
        low = total[span, :].astype(BF16)
        outer_grad[span, :] = low
        product = low.astype(F32) * attended[span, :]
        high = product.astype(BF16)
        rest = (product - high.astype(F32)).astype(BF16)
        delta = jnp.dot(high, head_of, preferred_element_type=F32)
        delta = delta + jnp.dot(rest, head_of, preferred_element_type=F32)
        own_stats[span, :] = lse[span, :] + delta

    by_rows(delta_part)
    payload[0:SEG, :] = outer_grad[0:SEG, :]
    mem_grad[...] = outer_grad[SEG:OWN, :]
    stats = jnp.transpose(own_stats[0:SEG, :])[0:STAT]
    high = stats.astype(BF16)
    rest = (stats - high.astype(F32)).astype(BF16)
    both = jnp.concatenate([high.astype(F32), rest.astype(F32)], 0).astype(BF16)
    payload[SEG : SEG + 2 * STAT, 0:SEG] = both
    payload[SEG : SEG + 2 * STAT, SEG:width] = jnp.zeros((2 * STAT, width - SEG), BF16)
    mem_stats[...] = jnp.transpose(own_stats[OWN - PAIR : OWN, :])[0:STAT]


def middle(meta, attended, lse, tokens, memory, token_cot, memory_cot, weights):
    wo, bo, gain1, shift1, wi, bi, w2, b2, gain2, shift2 = weights
    width, inner_width = wi.shape
    vmem, line = pl.BlockSpec(memory_space=pltpu.VMEM), lambda value: value.reshape(1, -1)
    hbm = pl.BlockSpec(memory_space=pl.ANY)
    shape = jax.ShapeDtypeStruct
    return pl.pallas_call(
        middle_body,
        in_specs=[pl.BlockSpec(memory_space=pltpu.SMEM)] + [vmem] * 14 + [hbm] * 2,
        out_specs=[vmem] * 16,
        out_shape=[
            shape((SEG, width), BF16),
            shape((MEMP, width), BF16),
            shape((SEG + 2 * STAT, width), BF16),
            shape((MEMP, width), BF16),
            shape((STAT, PAIR), F32),
            shape((OWN, PAIR), F32),
            shape((OWN, width), F32),
            shape((OWN, width), BF16),
            shape((OWN, width), BF16),
            shape((OWN, width), BF16),
            shape((OWN, width), BF16),
            shape((OWN, inner_width), BF16),
            shape((OWN, inner_width), BF16),
            shape((OWN, width), BF16),
            shape((8, width), F32),
            shape((1, inner_width), F32),
        ],
        scratch_shapes=[
            pltpu.VMEM((width, inner_width), BF16),
            pltpu.VMEM((inner_width, width), BF16),
            pltpu.VMEM((OWN, width), F32),
            pltpu.VMEM((OWN, width), F32),
            pltpu.VMEM((OWN, PAIR), F32),
            pltpu.VMEM((OWN, width), F32),
            pltpu.VMEM((OWN, width), F32),
            pltpu.VMEM((OWN, width), BF16),
            pltpu.VMEM((OWN, inner_width), F32),
            pltpu.VMEM((OWN, width), BF16),
            pltpu.SemaphoreType.DMA((2,)),
        ],
        compiler_params=pltpu.CompilerParams(vmem_limit_bytes=VMEM_LIMIT),
        cost_estimate=pl.CostEstimate(
            flops=12_000_000_000, bytes_accessed=40_000_000, transcendentals=2_000_000
        ),
        name="middle",
    )(
        meta, attended, lse, tokens, memory, token_cot, memory_cot,
        wo, line(bo), line(gain1), line(shift1), line(bi), line(b2), line(gain2), line(shift2),
        wi, w2,
    )


def late_body(metas, group, *refs, batches, chains, parts):
    refs = list(refs)
    take = lambda count: [refs.pop(0) for _ in range(count)]
    rows, res_mem = take(batches), take(batches)
    grads = [[take(len(parts[b])) for _ in range(3)] for b in range(batches)]
    weights = take(3)
    out, masked = take(2)
    width = weights[0].shape[0]
    out[3 * width :, :] = jnp.zeros((out.shape[0] - 3 * width, width), BF16)
    for b in range(batches):
        lead = jnp.where(metas[b, M_SPOT] == 0, 1.0, 0.0)
        masked[b, 0:SEG, :] = rows[b][0:SEG, :]
        masked[b, SEG:OWN, :] = rows[b][SEG:OWN, :] * lead.astype(BF16)
        grad = res_mem[b][SEG:OWN, :]
        for k in range(3):
            first = 0
            for part, ref in zip(parts[b], grads[b][k]):
                grad = grad + turned(ref[SEG:OWN, :], weights[k][:, first : first + part])
                first += part
        place = ((group[0] * batches + b) * chains + metas[b, M_CHAIN]) * MEMP
        place = pl.multiple_of(3 * width + place, MEMP)
        out[pl.ds(place, MEMP), :] = (grad * lead).astype(BF16)
    cuts = sorted({sum(p[:i]) for p in parts for i in range(len(p) + 1)})
    for k in range(3):
        for low, high in zip(cuts[:-1], cuts[1:]):
            total, line = None, None
            for b in range(batches):
                lead = jnp.where(metas[b, M_SPOT] == 0, 1.0, 0.0)
                first = 0
                for part, ref in zip(parts[b], grads[b][k]):
                    if first <= low and high <= first + part:
                        grad = ref[:, low - first : high - first]
                    first += part
                value = crossed(masked[b], grad)
                total = value if total is None else total + value
                if k != 1:
                    grad = grad.astype(F32)
                    value = jnp.sum(grad[0:SEG], 0, keepdims=True)
                    value = value + jnp.sum(grad[SEG:OWN], 0, keepdims=True) * lead
                    line = value if line is None else line + value
            out[k * width : (k + 1) * width, low:high] = total.astype(BF16)
            if k != 1:
                row = lax.broadcasted_iota(jnp.int32, (16, high - low), 0)
                span = slice(3 * width + MEMP - 16, 3 * width + MEMP)
                old = out[span, low:high].astype(F32)
                line_row = 16 - 2 + k // 2
                out[span, low:high] = jnp.where(row == line_row, line, old).astype(BF16)


def late_sums(metas, group, groups, chains, rows, res, grads, weights):
    batches, width = len(rows), weights[0].shape[0]
    parts = [[part.shape[1] for part in one[0]] for one in grads]
    count = 3 * width + groups * batches * chains * MEMP
    count += -count % LATE_ROWS
    vmem, smem = pl.BlockSpec(memory_space=pltpu.VMEM), pl.BlockSpec(memory_space=pltpu.SMEM)
    flat = [part for one in grads for name in one for part in name]
    return pl.pallas_call(
        functools.partial(late_body, batches=batches, chains=chains, parts=parts),
        in_specs=[smem] * 2 + [vmem] * (2 * batches + len(flat) + 3),
        out_specs=vmem,
        out_shape=jax.ShapeDtypeStruct((count, width), BF16),
        scratch_shapes=[pltpu.VMEM((batches, OWN, width), BF16)],
        compiler_params=pltpu.CompilerParams(vmem_limit_bytes=VMEM_LIMIT),
        name="late_sums",
    )(metas, group.reshape(1), *rows, *res, *flat, *weights)


def weight_grad(left, right):
    return lax.dot_general(left, right, (((0,), (0,)), ((), ())), preferred_element_type=F32)


def swap(value, mask):
    sizes = lax.axis_size("dp") * lax.axis_size("blk")
    return lax.ppermute(value, ("dp", "blk"), [(i, i ^ mask) for i in range(sizes)])


def sum_everywhere(value):
    blk = lax.axis_size("blk")
    place = lax.axis_index("dp") * blk + lax.axis_index("blk")
    groups = [(1,), (2, blk), (4, 8)]
    bit = 2 * blk
    while bit < blk * lax.axis_size("dp"):
        groups.append((bit,))
        bit *= 2
    masks_of = lambda group: [
        sum(bit for i, bit in enumerate(group) if (k >> i) & 1) for k in range(1 << len(group))
    ]
    own_of = lambda group: sum(((place // bit) % 2) << i for i, bit in enumerate(group))
    for group in groups:
        masks, own = masks_of(group), own_of(group)
        size = value.shape[0] // len(masks)
        part = lambda k: lax.dynamic_slice_in_dim(value, (own ^ k) * size, size)
        got = [swap(part(k), mask) for k, mask in enumerate(masks) if k]
        value = sum((g.astype(F32) for g in got), part(0).astype(F32)).astype(BF16)
    for group in reversed(groups):
        masks, own = masks_of(group), own_of(group)
        size = value.shape[0]
        got = [value] + [swap(value, mask) for mask in masks[1:]]
        value = jnp.zeros((size * len(masks), value.shape[1]), BF16)
        for k, part in enumerate(got):
            value = lax.dynamic_update_slice_in_dim(value, part, (own ^ k) * size, 0)
    return value


def local(
    tokens, memory, chain_lengths, last_fill,
    query_proj, query_bias, key_proj, value_proj, value_bias, output_proj, output_bias,
    attn_gain, attn_shift, inner_proj, inner_bias, outer_proj, outer_bias,
    final_gain, final_shift, token_cotangent, memory_cotangent,
):
    own = lax.axis_index("blk").astype(jnp.int32)
    group = lax.axis_index("dp").astype(jnp.int32)
    groups = lax.axis_size("dp")
    batches, _, width = tokens.shape
    chains, mem_rows = memory.shape[1:3]
    pad_mem = ((0, 0), (0, 0), (0, MEMP - mem_rows), (0, 0))
    memory, memory_cotangent = jnp.pad(memory, pad_mem), jnp.pad(memory_cotangent, pad_mem)

    metas = metas_of(own, chain_lengths[:, 0], last_fill[:, 0], mem_rows)
    near, (later, metas) = gather_near(tokens[0], ([tokens[b] for b in range(1, batches)], metas))
    later, near = lax.optimization_barrier((later, near))
    pieces = [near] + [gather_all(part) for part in later]
    meta_of = [metas[b] for b in range(batches)]

    states = []
    for b in range(batches):
        meta = meta_of[b]
        attended, lse, *chain_rows = attend_forward(
            meta, pieces[b], memory[b], (query_proj, query_bias, key_proj, value_proj, value_bias)
        )
        (
            final, final_mem, payload, mem_grad, mem_stats, own_stats, res_grad, rows,
            attended_low, branch, first_low, inner, active, outer, sums, inner_sum,
        ) = middle(
            meta, attended, lse, tokens[b], memory[b], token_cotangent[b], memory_cotangent[b],
            (
                output_proj, output_bias, attn_gain, attn_shift, inner_proj, inner_bias,
                outer_proj, outer_bias, final_gain, final_shift,
            ),
        )
        if b + 1 < batches:
            meta_of[b + 1], payload = lax.optimization_barrier((meta_of[b + 1], payload))
        states.append(
            dict(
                meta=meta, rows=rows, chain_rows=chain_rows, payload=payload, mem_grad=mem_grad,
                mem_stats=mem_stats, own_stats=own_stats, res_grad=res_grad, final=final,
                final_mem=final_mem, attended_low=attended_low, branch=branch,
                first_low=first_low, inner=inner, active=active, outer=outer, sums=sums,
                inner_sum=inner_sum,
            )
        )

    def over_batches(left, right):
        return weight_grad(
            jnp.concatenate([s[left] for s in states], 0),
            jnp.concatenate([s[right] for s in states], 0),
        ).astype(BF16)

    slots = (jnp.arange(groups)[:, None, None, None, None] == group) & (
        jnp.arange(chains)[:, None, None]
        == jnp.where(metas[:, M_SPOT] == 0, metas[:, M_CHAIN], -1)[:, None, None, None]
    )
    final_mem = jnp.stack([s["final_mem"] for s in states])[None, :, None]
    early = (
        over_batches("first_low", "inner"),
        over_batches("active", "outer"),
        over_batches("attended_low", "branch"),
        jnp.concatenate(
            [
                jnp.where(slots, final_mem, 0).astype(BF16).reshape(-1, width),
                sum(s["sums"] for s in states).astype(BF16),
                sum(s["inner_sum"] for s in states).astype(BF16).reshape(-1, width),
            ],
            0,
        ),
    )
    early, *held = lax.optimization_barrier((early, *[s["meta"] for s in states]))
    for s, meta in zip(states, held):
        s["meta"] = meta
        s["gathered"] = gather_all(s["payload"])
    def backward(s, meta):
        return attend_backward(
            meta, s["gathered"], s["chain_rows"], s["mem_grad"], s["mem_stats"],
            s["own_stats"], 0, NQUAD,
        )

    *others, last = states
    for s in others:
        s["grads"] = backward(s, s["meta"])
    got, last["gathered"], early = lax.optimization_barrier(
        ([s["grads"] for s in others], last["gathered"], early)
    )
    for s, grads in zip(others, got):
        s["grads"] = grads
    early = lax.psum(early, ("dp", "blk"))

    def late_part(turn, carry):
        grads = backward(last, last["meta"] + turn)
        every = [s["grads"] for s in others] + [grads]
        late = late_sums(
            metas, group, groups, chains, [s["rows"] for s in states],
            [s["res_grad"] for s in states], [[[part] for part in one] for one in every],
            (query_proj, key_proj, value_proj),
        )
        token_grads = []
        for s, one in zip(states, every):
            grad = s["res_grad"][:SEG]
            for part, weights in zip(one, (query_proj, key_proj, value_proj)):
                grad = grad + turned(part[:SEG], weights)
            token_grads.append(grad.astype(BF16))
        return sum_everywhere(late), token_grads

    once = jnp.minimum(metas[0, M_LEN], 1)
    start = jax.tree.map(
        lambda like: jnp.zeros(like.shape, like.dtype), jax.eval_shape(late_part, once, None)
    )
    late, token_grads = lax.fori_loop(0, once, late_part, start)
    late, early = lax.optimization_barrier((late, early))
    grad_inner, grad_outer, grad_output, rest = early

    def own_slots(rows):
        rows = rows.reshape(groups, batches, chains, MEMP, width)
        return lax.dynamic_index_in_dim(rows, group, keepdims=False)[:, :, :mem_rows]

    grad_query, grad_key, grad_value = (late[i * width : (i + 1) * width] for i in range(3))
    biases = late[3 * width + MEMP - 2 : 3 * width + MEMP].astype(F32)
    count = groups * batches * chains * MEMP
    memory_grad = own_slots(late[3 * width : 3 * width + count])
    memory_out = own_slots(rest[:count])
    sums, inner_sum = rest[count : count + 8], rest[count + 8 :].reshape(1, -1)
    token_outs = [s["final"] for s in states]

    wide = lambda value: value.astype(F32)
    return (
        jnp.stack(token_outs),
        memory_out,
        jnp.stack(token_grads),
        memory_grad,
        wide(grad_query),
        biases[0],
        wide(grad_key),
        wide(grad_value),
        biases[1],
        wide(grad_output),
        wide(sums[0]),
        wide(sums[1]),
        wide(sums[2]),
        wide(grad_inner),
        wide(inner_sum[0]),
        wide(grad_outer),
        wide(sums[3]),
        wide(sums[4]),
        wide(sums[5]),
    )


def solution(mesh):
    row_spec = P(None, ("dp", "blk"), None)
    mem_spec = P(None, "dp", None, None)
    int_spec = P(None, "dp", None)
    in_specs = (row_spec, mem_spec, int_spec, int_spec) + (P(),) * 15 + (row_spec, mem_spec)
    out_specs = (row_spec, mem_spec, row_spec, mem_spec) + (P(),) * 15
    return jax.shard_map(local, mesh=mesh, in_specs=in_specs, out_specs=out_specs, check_vma=False)
```

profile of v0, /device:TPU:0, one launch (start us, length us, event | category | flops | bytes accessed | tf_op | source)
XLA Modules:
  0.0 761.7 jit_solution(4136591325894444188)
XLA Ops:
  9.7 5.1 collective-permute-start.14
  19.1 12.4 %collective-permute-done.14.refs_2_ = bf16[512,768]{1,0:T(8,128)(2,1)S(1)} collective-permute-done((bf16[512,768]{1,0:T(8,128)(2,1)S(1)}, bf16[512,768]{1,0:T(8,128)(2,1)S(1)}, u32[]{:S(2)}, u32[]{:S(2)}) %collective-permute-start.14) | collective-permute-done | bytes 786464 | tf_op jit(solution)/shard_map/ppermute | solution.py:56
  37.7 4.6 collective-permute-start.17
  43.6 14.6 %collective-permute-done.19 = bf16[512,768]{1,0:T(8,128)(2,1)S(1)} collective-permute-done((bf16[512,768]{1,0:T(8,128)(2,1)S(1)}, bf16[512,768]{1,0:T(8,128)(2,1)S(1)}, u32[]{:S(2)}, u32[]{:S(2)}) %collective-permute-start.19) | collective-permute-done | bytes 786464 | tf_op jit(solution)/shard_map/ppermute | solution.py:56
  59.6 13.2 %collective-permute-done.18.refs_5_ = bf16[512,768]{1,0:T(8,128)(2,1)S(1)} collective-permute-done((bf16[512,768]{1,0:T(8,128)(2,1)}, bf16[512,768]{1,0:T(8,128)(2,1)S(1)}, u32[]{:S(2)}, u32[]{:S(2)}) %collective-permute-start.18) | collective-permute-done | bytes 786464 | tf_op jit(solution)/shard_map/ppermute | solution.py:56
  85.9 30.7 %attend_forward.2 = (f32[544,768]{1,0:T(8,128)}, f32[544,128]{1,0:T(8,128)}, bf16[4096,768]{1,0:T(8,128)(2,1)}, bf16[4096,768]{1,0:T(8,128)(2,1)}, bf16[4096,768]{1,0:T(8,128)(2,1)}) custom-call(s32[16]{0:T(128)} %get-tuple-element.532.meta, bf16[512,768]{1,0:T(8,128)(2,1)} %copy-done.14, bf16[512,768]{1,0:T(8,128)(2,1)} %collective-permute-done.15.refs_1_, ...), custom_call_target="tpu_custom_call" | custom-call | flops 40000000000 | bytes 30000000 | tf_op jit(solution)/shard_map/attend_forward/pallas_call | solution.py:293
  116.6 31.3 %middle.2 = (bf16[512,768]{1,0:T(8,128)(2,1)}, bf16[32,768]{1,0:T(8,128)(2,1)}, bf16[560,768]{1,0:T(8,128)(2,1)}, bf16[32,768]{1,0:T(8,128)(2,1)}, f32[24,128]{1...) custom-call(s32[16]{0:T(128)} %get-tuple-element.532.meta, ...), custom_call_target="tpu_custom_call" | custom-call | flops 12000000000 | bytes 40000000 | tf_op jit(solution)/shard_map/middle/pallas_call | solution.py:640
  148.0 31.4 %all-gather.7.cloned.1.call-done = bf16[8192,768]{1,0:T(8,128)(2,1)} async-done(((bf16[512,768]{1,0:T(8,128)(2,1)}), bf16[8192,768]{1,0:T(8,128)(2,1)}) %all-gather.7.cloned.1.call-update) | async-done | bytes 12582928 | tf_op jit(solution)/shard_map/all_gather | solution.py:70
  179.4 50.9 %attend_forward.3 = (f32[544,768]{1,0:T(8,128)}, f32[544,128]{1,0:T(8,128)}, bf16[4096,768]{1,0:T(8,128)(2,1)}, bf16[4096,768]{1,0:T(8,128)(2,1)}, bf16[4096,768]{1,0:T(8,128)(2,1)}) custom-call(s32[16]{0:T(128)S(1)} %get-tuple-element.841.meta, bf16[16,512,768]{2,1,0:T(8,128)(2,1)} %bitcast.76, bf16[4,32,768]{2,1,0:T(8,128)(2,1)} %get-tuple-element.655.refs_1_.memory, ...), custom_call_target="tpu_custom_call" | custom-call | flops 40000000000 | bytes 30000000 | tf_op jit(solution)/shard_map/attend_forward/pallas_call | solution.py:293
  230.3 29.1 %middle.3 = (bf16[512,768]{1,0:T(8,128)(2,1)}, bf16[32,768]{1,0:T(8,128)(2,1)}, bf16[560,768]{1,0:T(8,128)(2,1)}, bf16[32,768]{1,0:T(8,128)(2,1)S(1)}, f32[24,12...) custom-call(s32[16]{0:T(128)S(1)} %get-tuple-element.841.meta, ...), custom_call_target="tpu_custom_call" | custom-call | flops 12000000000 | bytes 40000000 | tf_op jit(solution)/shard_map/middle/pallas_call | solution.py:640
  269.1 8.0 %fusion.16 = bf16[768,3072]{1,0:T(8,128)(2,1)} fusion(bf16[544,3072]{1,0:T(8,128)(2,1)S(1)} %copy-done.41, bf16[544,3072]{1,0:T(8,128)(2,1)S(1)} %copy-done.40, bf16[544,768]{1,0:T(8,128)(2,1)S(1)} %copy-done.46, bf16[544,768]{1,0:T(8,128)(2,1)S(1)} %copy-done.45), kind=kOutput, calls=%fused_computation.36 | convolution fusion | flops 5152899072 | bytes 13074432 | tf_op jit(solution)/shard_map/dot_general | solution.py:755
  277.1 8.2 %fusion.13 = bf16[3072,768]{1,0:T(8,128)(2,1)} fusion(bf16[544,3072]{1,0:T(8,128)(2,1)S(1)} %copy-done.48, bf16[544,3072]{1,0:T(8,128)(2,1)S(1)} %copy-done.47, bf16[544,768]{1,0:T(8,128)(2,1)S(1)} %copy-done.50, bf16[544,768]{1,0:T(8,128)(2,1)S(1)} %copy-done.49), kind=kOutput, calls=%fused_computation.35 | convolution fusion | flops 5152899072 | bytes 13074432 | tf_op jit(solution)/shard_map/dot_general | solution.py:755
  288.0 19.2 %all-gather.9.cloned.1.call-done = bf16[8960,768]{1,0:T(8,128)(2,1)} async-done(((bf16[560,768]{1,0:T(8,128)(2,1)}), bf16[8960,768]{1,0:T(8,128)(2,1)}) %all-gather.9.cloned.1.call-update) | async-done | bytes 13762576 | tf_op jit(solution)/shard_map/all_gather | solution.py:70
  307.1 41.0 %attend_backward.6 = (bf16[544,768]{1,0:T(8,128)(2,1)}, bf16[544,768]{1,0:T(8,128)(2,1)}, bf16[544,768]{1,0:T(8,128)(2,1)}) custom-call(s32[16]{0:T(128)} %get-tuple-element.532.meta, bf16[16,560,768]{2,1,0:T(8,128)(2,1)} %bitcast.75, bf16[4096,768]{1,0:T(8,128)(2,1)} %get-tuple-element.534.refs_1_, bf16[4096,768]{1,0:T(8,128)(2,1)} %get-tuple-element.535.refs_2_, ...), custom_call_target="tpu_custom_call" | custom-call | flops 10000000000 | bytes 1000000 | tf_op jit(solution)/shard_map/attend_backward/pallas_call | solution.py:434
  348.2 68.5 %all-gather.11.cloned.1.call-done = bf16[8960,768]{1,0:T(8,128)(2,1)} async-done(((bf16[560,768]{1,0:T(8,128)(2,1)}), bf16[8960,768]{1,0:T(8,128)(2,1)}) %all-gather.11.cloned.1.call-update) | async-done | bytes 13762576 | tf_op jit(solution)/shard_map/all_gather | solution.py:70
  422.3 4.3 add_convert_fusion.4
  430.8 298.4 %while.17 = (s32[]{:T(128)}, bf16[2816,768]{1,0:T(8,128)(2,1)}, bf16[512,768]{1,0:T(8,128)(2,1)}, bf16[512,768]{1,0:T(8,128)(2,1)}, s32[]{:T(128)}, /*index=5*/s...) while((s32[]{:T(128)}, bf16[2816,768]{1,0:T(8,128)(2,1)}, ...), condition=%wide.region_1.2_spmd, body=%wide.region_0.1_spmd.sunk | while | flops 11820540928 | bytes 134147560 | solution.py:903
  447.1 65.7 %attend_backward.7 = (bf16[544,768]{1,0:T(8,128)(2,1)}, bf16[544,768]{1,0:T(8,128)(2,1)}, bf16[544,768]{1,0:T(8,128)(2,1)}) custom-call(s32[16]{0:T(128)} %broadcast_add_fusion.2.meta, bf16[16,560,768]{2,1,0:T(8,128)(2,1)} %get-tuple-element.928.refs_0_, bf16[4096,768]{1,0:T(8,128)(2,1)} %get-tuple-element.929.refs_1_, ...), custom_call_target="tpu_custom_call" | custom-call | flops 10000000000 | bytes 1000000 | tf_op jit(solution)/shard_map/while/body/attend_backward/pallas_call | solution.py:434
  512.8 14.0 %late_sums.5 = bf16[2816,768]{1,0:T(8,128)(2,1)} custom-call(s32[2,16]{1,0:T(2,128)S(1)} %get-tuple-element.935.metas, s32[1]{0:T(128)} %bitcast.57.group, bf16[544,768]{1,0:T(8,128)(2,1)} %get-tuple-element.936.refs_0_, bf16[544,768]{1,0:T(8,128)(2,1)} %get-tuple-element.937.refs_1_, f32[544,768]{1,0:T(8,128)} %get-tuple-element.938.refs_2_, ...), custom_call_target="tpu_custom_call" | custom-call | tf_op jit(solution)/shard_map/while/body/late_sums/pallas_call | solution.py:743
  537.2 42.0 %collective-permute-start.1 = (bf16[352,768]{1,0:T(8,128)(2,1)}, bf16[352,768]{1,0:T(8,128)(2,1)}, u32[]{:S(2)}, u32[]{:S(2)}) collective-permute-start(bf16[352,768]{1,0:T(8,128)(2,1)} %get-tuple-element.827), channel_id=1, source_target_pairs={{0,18},{1,19},{2,16},{3,17},{4,22},{5,23},{6,20},{7,21},{8,26},{9,... | collective-permute-start | bytes 1622024 | tf_op jit(solution)/shard_map/while/body/ppermute | solution.py:760
  580.4 12.2 %collective-permute-done.1 = bf16[352,768]{1,0:T(8,128)(2,1)} collective-permute-done((bf16[352,768]{1,0:T(8,128)(2,1)}, bf16[352,768]{1,0:T(8,128)(2,1)}, u32[]{:S(2)}, u32[]{:S(2)}) %collective-permute-start.1) | collective-permute-done | bytes 540704 | tf_op jit(solution)/shard_map/while/body/ppermute | solution.py:760
  592.6 18.1 %collective-permute-done.2 = bf16[352,768]{1,0:T(8,128)(2,1)} collective-permute-done((bf16[352,768]{1,0:T(8,128)(2,1)}, bf16[352,768]{1,0:T(8,128)(2,1)}, u32[]{:S(2)}, u32[]{:S(2)}) %collective-permute-start.2) | collective-permute-done | bytes 540704 | tf_op jit(solution)/shard_map/while/body/ppermute | solution.py:760
  616.0 19.6 %collective-permute-start.4 = (bf16[88,768]{1,0:T(8,128)(2,1)S(1)}, bf16[88,768]{1,0:T(8,128)(2,1)S(1)}, u32[]{:S(2)}, u32[]{:S(2)}) collective-permute-start(bf16[88,768]{1,0:T(8,128)(2,1)S(1)} %get-tuple-element.830), channel_id=1, source_target_pairs={{0,12},{1,13},{2,14},{3,15},{4,8},{5,9},{6,10},{7,11},{8,4},{9,5},... | collective-permute-start | bytes 405512 | tf_op jit(solution)/shard_map/while/body/ppermute | solution.py:760
  635.5 6.9 collective-permute-start.5
  642.5 15.0 %collective-permute-done.5 = bf16[88,768]{1,0:T(8,128)(2,1)S(1)} collective-permute-done((bf16[88,768]{1,0:T(8,128)(2,1)S(1)}, bf16[88,768]{1,0:T(8,128)(2,1)S(1)}, u32[]{:S(2)}, u32[]{:S(2)}) %collective-permute-start.5) | collective-permute-done | bytes 135200 | tf_op jit(solution)/shard_map/while/body/ppermute | solution.py:760
  662.9 6.3 collective-permute-done.7
  672.2 5.3 collective-permute-done.9
  681.9 20.8 %collective-permute-done.10 = bf16[352,768]{1,0:T(8,128)(2,1)S(1)} collective-permute-done((bf16[352,768]{1,0:T(8,128)(2,1)S(1)}, bf16[352,768]{1,0:T(8,128)(2,1)S(1)}, u32[]{:S(2)}, u32[]{:S(2)}) %collective-permute-start.10) | collective-permute-done | bytes 540704 | tf_op jit(solution)/shard_map/while/body/ppermute | solution.py:760
  706.4 9.0 %collective-permute-done.12 = bf16[352,768]{1,0:T(8,128)(2,1)S(1)} collective-permute-done((bf16[352,768]{1,0:T(8,128)(2,1)S(1)}, bf16[352,768]{1,0:T(8,128)(2,1)S(1)}, u32[]{:S(2)}, u32[]{:S(2)}) %collective-permute-start.12) | collective-permute-done | bytes 540704 | tf_op jit(solution)/shard_map/while/body/ppermute | solution.py:760
  731.9 5.3 slice_convert_fusion
  740.2 5.0 convert_element_type.203
  745.2 4.5 convert_element_type.206
  (237 shorter events, 108.1 us)
Async XLA Ops:
  7.2 172.2 %all-gather.7.cloned.1.call-start = ((), (), s32[]{:S(2)}) async-start(), calls=%async_computation | async-start | bytes 13369344 | tf_op jit(solution)/shard_map/all_gather | solution.py:70
  9.7 21.8 %collective-permute-start.14 = (bf16[512,768]{1,0:T(8,128)(2,1)S(1)}, bf16[512,768]{1,0:T(8,128)(2,1)S(1)}, u32[]{:S(2)}, u32[]{:S(2)}) collective-permute-start(bf16[512,768]{1,0:T(8,128)(2,1)S(1)} %get-tuple-element.490.refs_0_.tokens), channel_id=1, source_target_pairs={{0,4},{1,5},{2,6},{3,7},{4,8},{5,9},{6,10},{7,11},{8,12},{9,13},{1... | collective-permute-start | bytes 2359304 | tf_op jit(solution)/shard_map/ppermute | solution.py:56
  14.8 20.9 %collective-permute-start.16 = (bf16[512,768]{1,0:T(8,128)(2,1)S(1)}, bf16[512,768]{1,0:T(8,128)(2,1)S(1)}, u32[]{:S(2)}, u32[]{:S(2)}) collective-permute-start(bf16[512,768]{1,0:T(8,128)(2,1)S(1)} %get-tuple-element.490.refs_0_.tokens), channel_id=1, source_target_pairs={{4,0},{5,1},{6,2},{7,3},{8,4},{9,5},{10,6},{11,7},{12,8},{13,9},{1... | collective-permute-start | bytes 2359304 | tf_op jit(solution)/shard_map/ppermute | solution.py:56
  16.1 21.6 %collective-permute-start.15 = (bf16[512,768]{1,0:T(8,128)(2,1)S(1)}, bf16[512,768]{1,0:T(8,128)(2,1)}, u32[]{:S(2)}, u32[]{:S(2)}) collective-permute-start(bf16[512,768]{1,0:T(8,128)(2,1)S(1)} %get-tuple-element.490.refs_0_.tokens), channel_id=1, source_target_pairs={{0,2},{1,3},{2,0},{3,1},{4,6},{5,7},{6,4},{7,5},{8,10},{9,11},{10,... | collective-permute-start | bytes 2359304 | tf_op jit(solution)/shard_map/ppermute | solution.py:56
  35.8 22.4 %collective-permute-start.19 = (bf16[512,768]{1,0:T(8,128)(2,1)S(1)}, bf16[512,768]{1,0:T(8,128)(2,1)S(1)}, u32[]{:S(2)}, u32[]{:S(2)}) collective-permute-start(bf16[512,768]{1,0:T(8,128)(2,1)S(1)} %broadcast_select_fusion), channel_id=1, source_target_pairs={{2,6},{3,7},{4,0},{5,1},{6,10},{7,11},{8,4},{9,5},{10,14},{11,15},... | collective-permute-start | bytes 2359304 | tf_op jit(solution)/shard_map/ppermute | solution.py:56
  37.1 21.6 %collective-permute-start.21 = (bf16[512,768]{1,0:T(8,128)(2,1)S(1)}, bf16[512,768]{1,0:T(8,128)(2,1)S(1)}, u32[]{:S(2)}, u32[]{:S(2)}) collective-permute-start(bf16[512,768]{1,0:T(8,128)(2,1)S(1)} %get-tuple-element.490.refs_0_.tokens), channel_id=1, source_target_pairs={{0,1},{1,0},{2,3},{3,2},{4,5},{5,4},{6,7},{7,6},{8,9},{9,8},{10,11... | collective-permute-start | bytes 2359304 | tf_op jit(solution)/shard_map/ppermute | solution.py:56
  37.2 21.6 %collective-permute-start.23 = (bf16[512,768]{1,0:T(8,128)(2,1)S(1)}, bf16[512,768]{1,0:T(8,128)(2,1)S(1)}, u32[]{:S(2)}, u32[]{:S(2)}) collective-permute-start(bf16[512,768]{1,0:T(8,128)(2,1)S(1)} %collective-permute-done.14.refs_2_), channel_id=1, source_target_pairs={{0,1},{1,0},{2,3},{3,2},{4,5},{5,4},{6,7},{7,6},{8,9},{9,8},{10,11... | collective-permute-start | bytes 2359304 | tf_op jit(solution)/shard_map/ppermute | solution.py:56
  37.7 21.9 %collective-permute-start.17 = (bf16[512,768]{1,0:T(8,128)(2,1)}, bf16[512,768]{1,0:T(8,128)(2,1)S(1)}, u32[]{:S(2)}, u32[]{:S(2)}) collective-permute-start(bf16[512,768]{1,0:T(8,128)(2,1)} %collective-permute-done.15.refs_1_), channel_id=1, source_target_pairs={{0,4},{1,5},{2,6},{3,7},{4,8},{5,9},{6,10},{7,11},{8,12},{9,13},{1... | collective-permute-start | bytes 2359304 | tf_op jit(solution)/shard_map/ppermute | solution.py:56
  42.3 30.5 %collective-permute-start.18 = (bf16[512,768]{1,0:T(8,128)(2,1)}, bf16[512,768]{1,0:T(8,128)(2,1)S(1)}, u32[]{:S(2)}, u32[]{:S(2)}) collective-permute-start(bf16[512,768]{1,0:T(8,128)(2,1)} %collective-permute-done.15.refs_1_), channel_id=1, source_target_pairs={{4,0},{5,1},{6,2},{7,3},{8,4},{9,5},{10,6},{11,7},{12,8},{13,9},{1... | collective-permute-start | bytes 2359304 | tf_op jit(solution)/shard_map/ppermute | solution.py:56
  58.2 15.0 %collective-permute-start.20 = (bf16[512,768]{1,0:T(8,128)(2,1)S(1)}, bf16[512,768]{1,0:T(8,128)(2,1)S(1)}, u32[]{:S(2)}, u32[]{:S(2)}) collective-permute-start(bf16[512,768]{1,0:T(8,128)(2,1)S(1)} %collective-permute-done.19), channel_id=1, source_target_pairs={{0,2},{1,3},{2,0},{3,1},{4,6},{5,7},{6,4},{7,5},{8,10},{9,11},{10,... | collective-permute-start | bytes 2359304 | tf_op jit(solution)/shard_map/ppermute | solution.py:56
  58.7 14.5 %collective-permute-start.22 = (bf16[512,768]{1,0:T(8,128)(2,1)}, bf16[512,768]{1,0:T(8,128)(2,1)S(1)}, u32[]{:S(2)}, u32[]{:S(2)}) collective-permute-start(bf16[512,768]{1,0:T(8,128)(2,1)} %collective-permute-done.15.refs_1_), channel_id=1, source_target_pairs={{0,1},{1,0},{2,3},{3,2},{4,5},{5,4},{6,7},{7,6},{8,9},{9,8},{10,11... | collective-permute-start | bytes 2359304 | tf_op jit(solution)/shard_map/ppermute | solution.py:56
  58.8 14.5 %collective-permute-start.24 = (bf16[512,768]{1,0:T(8,128)(2,1)S(1)}, bf16[512,768]{1,0:T(8,128)(2,1)S(1)}, u32[]{:S(2)}, u32[]{:S(2)}) collective-permute-start(bf16[512,768]{1,0:T(8,128)(2,1)S(1)} %collective-permute-done.16.refs_3_), channel_id=1, source_target_pairs={{0,1},{1,0},{2,3},{3,2},{4,5},{5,4},{6,7},{7,6},{8,9},{9,8},{10,11... | collective-permute-start | bytes 2359304 | tf_op jit(solution)/shard_map/ppermute | solution.py:56
  59.6 13.7 %collective-permute-start.25 = (bf16[512,768]{1,0:T(8,128)(2,1)S(1)}, bf16[512,768]{1,0:T(8,128)(2,1)S(1)}, u32[]{:S(2)}, u32[]{:S(2)}) collective-permute-start(bf16[512,768]{1,0:T(8,128)(2,1)S(1)} %collective-permute-done.17.refs_4_), channel_id=1, source_target_pairs={{0,1},{1,0},{2,3},{3,2},{4,5},{5,4},{6,7},{7,6},{8,9},{9,8},{10,11... | collective-permute-start | bytes 2359304 | tf_op jit(solution)/shard_map/ppermute | solution.py:56
  72.8 2.3 collective-permute-start.26
  73.2 3.1 collective-permute-start.27
  76.3 230.8 %all-gather.9.cloned.1.call-start = ((), (), s32[]{:S(2)}) async-start(), calls=%async_computation.1 | async-start | bytes 14622720 | tf_op jit(solution)/shard_map/all_gather | solution.py:70
  148.0 268.7 %all-gather.11.cloned.1.call-start = ((), (), s32[]{:S(2)}) async-start(), calls=%async_computation.2 | async-start | bytes 14622720 | tf_op jit(solution)/shard_map/all_gather | solution.py:70
  259.5 472.4 %all-reduce.5.cloned.1.call-start = ((), (), s32[]{:S(2)}) async-start(), calls=%async_computation.3 | async-start | bytes 22855680 | tf_op jit(solution)/shard_map/psum | solution.py:881
  528.6 4.5 collective-permute-start
  537.2 55.4 %collective-permute-start.1 = (bf16[352,768]{1,0:T(8,128)(2,1)}, bf16[352,768]{1,0:T(8,128)(2,1)}, u32[]{:S(2)}, u32[]{:S(2)}) collective-permute-start(bf16[352,768]{1,0:T(8,128)(2,1)} %get-tuple-element.827), channel_id=1, source_target_pairs={{0,18},{1,19},{2,16},{3,17},{4,22},{5,23},{6,20},{7,21},{8,26},{9,... | collective-permute-start | bytes 1622024 | tf_op jit(solution)/shard_map/while/body/ppermute | solution.py:760
  579.2 31.5 %collective-permute-start.2 = (bf16[352,768]{1,0:T(8,128)(2,1)}, bf16[352,768]{1,0:T(8,128)(2,1)}, u32[]{:S(2)}, u32[]{:S(2)}) collective-permute-start(bf16[352,768]{1,0:T(8,128)(2,1)} %get-tuple-element.828), channel_id=1, source_target_pairs={{0,16},{1,17},{2,18},{3,19},{4,20},{5,21},{6,22},{7,23},{8,24},{9,... | collective-permute-start | bytes 1622024 | tf_op jit(solution)/shard_map/while/body/ppermute | solution.py:760
  579.2 33.3 %collective-permute-start.3 = (bf16[352,768]{1,0:T(8,128)(2,1)}, bf16[352,768]{1,0:T(8,128)(2,1)}, u32[]{:S(2)}, u32[]{:S(2)}) collective-permute-start(bf16[352,768]{1,0:T(8,128)(2,1)} %get-tuple-element.829), channel_id=1, source_target_pairs={{0,2},{1,3},{2,0},{3,1},{4,6},{5,7},{6,4},{7,5},{8,10},{9,11},{10,... | collective-permute-start | bytes 1622024 | tf_op jit(solution)/shard_map/while/body/ppermute | solution.py:760
  616.0 26.5 %collective-permute-start.4 = (bf16[88,768]{1,0:T(8,128)(2,1)S(1)}, bf16[88,768]{1,0:T(8,128)(2,1)S(1)}, u32[]{:S(2)}, u32[]{:S(2)}) collective-permute-start(bf16[88,768]{1,0:T(8,128)(2,1)S(1)} %get-tuple-element.830), channel_id=1, source_target_pairs={{0,12},{1,13},{2,14},{3,15},{4,8},{5,9},{6,10},{7,11},{8,4},{9,5},... | collective-permute-start | bytes 405512 | tf_op jit(solution)/shard_map/while/body/ppermute | solution.py:760
  635.5 21.9 %collective-permute-start.5 = (bf16[88,768]{1,0:T(8,128)(2,1)S(1)}, bf16[88,768]{1,0:T(8,128)(2,1)S(1)}, u32[]{:S(2)}, u32[]{:S(2)}) collective-permute-start(bf16[88,768]{1,0:T(8,128)(2,1)S(1)} %get-tuple-element.831), channel_id=1, source_target_pairs={{0,8},{1,9},{2,10},{3,11},{4,12},{5,13},{6,14},{7,15},{8,0},{9,1},... | collective-permute-start | bytes 405512 | tf_op jit(solution)/shard_map/while/body/ppermute | solution.py:760
  642.5 15.0 %collective-permute-start.6 = (bf16[88,768]{1,0:T(8,128)(2,1)S(1)}, bf16[88,768]{1,0:T(8,128)(2,1)S(1)}, u32[]{:S(2)}, u32[]{:S(2)}) collective-permute-start(bf16[88,768]{1,0:T(8,128)(2,1)S(1)} %get-tuple-element.832), channel_id=1, source_target_pairs={{0,4},{1,5},{2,6},{3,7},{4,0},{5,1},{6,2},{7,3},{8,12},{9,13},{10,... | collective-permute-start | bytes 405512 | tf_op jit(solution)/shard_map/while/body/ppermute | solution.py:760
  658.5 10.8 %collective-permute-start.7 = (bf16[88,768]{1,0:T(8,128)(2,1)S(1)}, bf16[88,768]{1,0:T(8,128)(2,1)S(1)}, u32[]{:S(2)}, u32[]{:S(2)}) collective-permute-start(bf16[88,768]{1,0:T(8,128)(2,1)S(1)} %get-tuple-element.834), channel_id=1, source_target_pairs={{0,4},{1,5},{2,6},{3,7},{4,0},{5,1},{6,2},{7,3},{8,12},{9,13},{10,... | collective-permute-start | bytes 405512 | tf_op jit(solution)/shard_map/while/body/ppermute | solution.py:760
  658.5 13.6 %collective-permute-start.8 = (bf16[88,768]{1,0:T(8,128)(2,1)S(1)}, bf16[88,768]{1,0:T(8,128)(2,1)S(1)}, u32[]{:S(2)}, u32[]{:S(2)}) collective-permute-start(bf16[88,768]{1,0:T(8,128)(2,1)S(1)} %get-tuple-element.834), channel_id=1, source_target_pairs={{0,8},{1,9},{2,10},{3,11},{4,12},{5,13},{6,14},{7,15},{8,0},{9,1},... | collective-permute-start | bytes 405512 | tf_op jit(solution)/shard_map/while/body/ppermute | solution.py:760
  661.1 16.4 %collective-permute-start.9 = (bf16[88,768]{1,0:T(8,128)(2,1)S(1)}, bf16[88,768]{1,0:T(8,128)(2,1)S(1)}, u32[]{:S(2)}, u32[]{:S(2)}) collective-permute-start(bf16[88,768]{1,0:T(8,128)(2,1)S(1)} %get-tuple-element.834), channel_id=1, source_target_pairs={{0,12},{1,13},{2,14},{3,15},{4,8},{5,9},{6,10},{7,11},{8,4},{9,5},... | collective-permute-start | bytes 405512 | tf_op jit(solution)/shard_map/while/body/ppermute | solution.py:760
  677.5 25.2 %collective-permute-start.10 = (bf16[352,768]{1,0:T(8,128)(2,1)S(1)}, bf16[352,768]{1,0:T(8,128)(2,1)S(1)}, u32[]{:S(2)}, u32[]{:S(2)}) collective-permute-start(bf16[352,768]{1,0:T(8,128)(2,1)S(1)} %constant_dynamic-update-slice_fusion.23), channel_id=1, source_target_pairs={{0,2},{1,3},{2,0},{3,1},{4,6},{5,7},{6,4},{7,5},{8,10},{9,11},{10,... | collective-permute-start | bytes 1622024 | tf_op jit(solution)/shard_map/while/body/ppermute | solution.py:760
  680.2 26.1 %collective-permute-start.11 = (bf16[352,768]{1,0:T(8,128)(2,1)S(1)}, bf16[352,768]{1,0:T(8,128)(2,1)S(1)}, u32[]{:S(2)}, u32[]{:S(2)}) collective-permute-start(bf16[352,768]{1,0:T(8,128)(2,1)S(1)} %constant_dynamic-update-slice_fusion.23), channel_id=1, source_target_pairs={{0,16},{1,17},{2,18},{3,19},{4,20},{5,21},{6,22},{7,23},{8,24},{9,... | collective-permute-start | bytes 1622024 | tf_op jit(solution)/shard_map/while/body/ppermute | solution.py:760
  680.2 35.1 %collective-permute-start.12 = (bf16[352,768]{1,0:T(8,128)(2,1)S(1)}, bf16[352,768]{1,0:T(8,128)(2,1)S(1)}, u32[]{:S(2)}, u32[]{:S(2)}) collective-permute-start(bf16[352,768]{1,0:T(8,128)(2,1)S(1)} %constant_dynamic-update-slice_fusion.23), channel_id=1, source_target_pairs={{0,18},{1,19},{2,16},{3,17},{4,22},{5,23},{6,20},{7,21},{8,26},{9,... | collective-permute-start | bytes 1622024 | tf_op jit(solution)/shard_map/while/body/ppermute | solution.py:760
  715.4 9.5 %collective-permute-start.13 = (bf16[1408,768]{1,0:T(8,128)(2,1)S(1)}, bf16[1408,768]{1,0:T(8,128)(2,1)}, u32[]{:S(2)}, u32[]{:S(2)}) collective-permute-start(bf16[1408,768]{1,0:T(8,128)(2,1)S(1)} %constant_dynamic-update-slice_fusion.27), channel_id=1, source_target_pairs={{0,1},{1,0},{2,3},{3,2},{4,5},{5,4},{6,7},{7,6},{8,9},{9,8},{10,11... | collective-permute-start | bytes 6488072 | tf_op jit(solution)/shard_map/while/body/ppermute | solution.py:760
  (55 other events, 1325.2 us)
Sparse Core Ops, SparseCore 0:
  76.4 102.8 all-gather.6
  182.2 124.8 all-gather.8
  310.0 106.6 all-gather.10
  423.5 299.3 all-reduce.4
where the time goes:
time: 770 us; the launch traced here: 762 us
  waiting for transfers between devices  265 us (34%)
  Pallas kernels  264 us (34%)
  starting transfers between devices  95.8 us (12%)
  matrix products  36.6 us (5%)
  other arithmetic  34.3 us (4%)
  local copies, waits for them, and re-layouts  33.9 us (4%)
  loops' own time  16.1 us (2%)
  between operations  15.5 us (2%)
    all_gather x3, waiting for transfers between devices, gather_all(): return [lax.all_gather(value, 'blk')]  119 us
    pallas_call x2, Pallas kernels, attend_backward(): pl.pallas_call(functools.partial(backward_body, start, count), grid_spec=...  107 us
    ppermute x14, waiting for transfers between devices, swap(): lax.ppermute(value, ('dp', 'blk'), [(i, i ^ mask) for i in range(sizes)])  99 us
    pallas_call x2, Pallas kernels, attend_forward(): pl.pallas_call(forward_body, grid_spec=pltpu.PrefetchScalarGridSpec(num_s...  81.6 us
    ppermute x14, starting transfers between devices, swap(): lax.ppermute(value, ('dp', 'blk'), [(i, i ^ mask) for i in range(sizes)])  78.8 us
    pallas_call x2, Pallas kernels, middle(): pl.pallas_call(middle_body, in_specs=[pl.BlockSpec(memory_space=pltpu.SME...  60.5 us
    ppermute x14, waiting for transfers between devices, move(): return lax.ppermute(value, 'blk', pairs)  47.1 us
    dot_general x3, matrix products, weight_grad(): lax.dot_general(left, right, (((0,), (0,)), ((), ())), preferred_element_...  20.3 us
  transfers between devices with their start and end apart: 32, of which 22 were waited for; matrix products, arithmetic and copies ran while one was open for 9% of the time, Pallas kernels for 35%

commit v1 on v0

--- a/solution.py
+++ b/solution.py
@@ -760,7 +760,7 @@
     return lax.ppermute(value, ("dp", "blk"), [(i, i ^ mask) for i in range(sizes)])
 
 
-def sum_everywhere(value):
+def sum_everywhere(value, beside):
     blk = lax.axis_size("blk")
     place = lax.axis_index("dp") * blk + lax.axis_index("blk")
     groups = [(1,), (2, blk), (4, 8)]
@@ -777,6 +777,8 @@
         size = value.shape[0] // len(masks)
         part = lambda k: lax.dynamic_slice_in_dim(value, (own ^ k) * size, size)
         got = [swap(part(k), mask) for k, mask in enumerate(masks) if k]
+        if group == groups[1]:
+            got[-1], beside = lax.optimization_barrier((got[-1], beside))
         value = sum((g.astype(F32) for g in got), part(0).astype(F32)).astype(BF16)
     for group in reversed(groups):
         masks, own = masks_of(group), own_of(group)
@@ -785,7 +787,7 @@
         value = jnp.zeros((size * len(masks), value.shape[1]), BF16)
         for k, part in enumerate(got):
             value = lax.dynamic_update_slice_in_dim(value, part, (own ^ k) * size, 0)
-    return value
+    return value, beside
 
 
 def local(
@@ -882,7 +884,8 @@
 
     def late_part(turn, carry):
         grads = backward(last, last["meta"] + turn)
-        every = [s["grads"] for s in others] + [grads]
+        every, grads = lax.optimization_barrier(([s["grads"] for s in others], grads))
+        every = every + [grads]
         late = late_sums(
             metas, group, groups, chains, [s["rows"] for s in states],
             [s["res_grad"] for s in states], [[[part] for part in one] for one in every],
@@ -894,7 +897,7 @@
             for part, weights in zip(one, (query_proj, key_proj, value_proj)):
                 grad = grad + turned(part[:SEG], weights)
             token_grads.append(grad.astype(BF16))
-        return sum_everywhere(late), token_grads
+        return sum_everywhere(late, jnp.stack(token_grads))
 
     once = jnp.minimum(metas[0, M_LEN], 1)
     start = jax.tree.map(
@@ -920,7 +923,7 @@
     return (
         jnp.stack(token_outs),
         memory_out,
-        jnp.stack(token_grads),
+        token_grads,
         memory_grad,
         wide(grad_query),
         biases[0],

time: 770 us -> 757 us (0.983)
  Pallas kernels: 264 us -> 427 us
  waiting for transfers between devices: 265 us -> 142 us
  starting transfers between devices: 95.8 us -> 57.9 us
  matrix products: 36.6 us -> 28.2 us
    all_gather x3, waiting for transfers between devices: 119 us -> 0.04 us  [gather_all(): return [lax.all_gather(value, 'blk')]]
    pallas_call x2, Pallas kernels: 107 us -> 201 us  [attend_backward(): pl.pallas_call(functools.partial(backward_body, start, count), grid_spec=...]
    pallas_call x2, Pallas kernels: 81.6 us -> 151 us  [attend_forward(): pl.pallas_call(forward_body, grid_spec=pltpu.PrefetchScalarGridSpec(num_s...]
    ppermute x14, starting transfers between devices: 78.8 us -> 40.9 us  [swap(): lax.ppermute(value, ('dp', 'blk'), [(i, i ^ mask) for i in range(sizes)])]
    dot_general x6, matrix products: 16.3 us -> 7.9 us  [turned(): return lax.dot_general(left, right, LAST, preferred_element_type=F32)]
  transfers between devices with their start and end apart: 32 -> 32, of which waited for: 22 -> 21; matrix products, arithmetic and copies ran while one was open for 9% -> 8% of each run, Pallas kernels for 35% -> 57%
where the time goes in v1:
time: 757 us; the launch traced here: 748 us
  Pallas kernels  427 us (56%)
  waiting for transfers between devices  142 us (19%)
  starting transfers between devices  57.9 us (8%)
  local copies, waits for them, and re-layouts  31.2 us (4%)
  other arithmetic  29.2 us (4%)
  matrix products  28.2 us (4%)
  loops' own time  17.3 us (2%)
  between operations  15.5 us (2%)
    pallas_call x2, Pallas kernels, attend_backward(): pl.pallas_call(functools.partial(backward_body, start, count), grid_spec=...  201 us
    pallas_call x2, Pallas kernels, attend_forward(): pl.pallas_call(forward_body, grid_spec=pltpu.PrefetchScalarGridSpec(num_s...  151 us
    ppermute x14, waiting for transfers between devices, swap(): lax.ppermute(value, ('dp', 'blk'), [(i, i ^ mask) for i in range(sizes)])  93.3 us
    pallas_call x2, Pallas kernels, middle(): pl.pallas_call(middle_body, in_specs=[pl.BlockSpec(memory_space=pltpu.SME...  59.4 us
    ppermute x14, waiting for transfers between devices, move(): return lax.ppermute(value, 'blk', pairs)  47.2 us
    ppermute x14, starting transfers between devices, swap(): lax.ppermute(value, ('dp', 'blk'), [(i, i ^ mask) for i in range(sizes)])  40.9 us
    dot_general x3, matrix products, weight_grad(): lax.dot_general(left, right, (((0,), (0,)), ((), ())), preferred_element_...  20.3 us
    another operation x1, loops' own time, local(): late, token_grads = lax.fori_loop(0, once, late_part, start)  17.3 us
  transfers between devices with their start and end apart: 32, of which 21 were waited for; matrix products, arithmetic and copies ran while one was open for 8% of the time, Pallas kernels for 57%

profile of v1, /device:TPU:0, one launch (start us, length us, event | category | flops | bytes accessed | tf_op | source)
XLA Modules:
  0.0 748.2 jit_solution(14548077092827902827)
XLA Ops:
  9.7 5.1 collective-permute-start.14
  19.1 12.4 %collective-permute-done.14.refs_2_ = bf16[512,768]{1,0:T(8,128)(2,1)S(1)} collective-permute-done((bf16[512,768]{1,0:T(8,128)(2,1)S(1)}, bf16[512,768]{1,0:T(8,128)(2,1)S(1)}, u32[]{:S(2)}, u32[]{:S(2)}) %collective-permute-start.14) | collective-permute-done | bytes 786464 | tf_op jit(solution)/shard_map/ppermute | solution.py:56
  31.5 4.2 collective-permute-done.16.refs_3_
  37.7 4.6 collective-permute-start.17
  43.6 14.6 %collective-permute-done.19 = bf16[512,768]{1,0:T(8,128)(2,1)S(1)} collective-permute-done((bf16[512,768]{1,0:T(8,128)(2,1)S(1)}, bf16[512,768]{1,0:T(8,128)(2,1)S(1)}, u32[]{:S(2)}, u32[]{:S(2)}) %collective-permute-start.19) | collective-permute-done | bytes 786464 | tf_op jit(solution)/shard_map/ppermute | solution.py:56
  59.6 13.2 %collective-permute-done.18.refs_5_ = bf16[512,768]{1,0:T(8,128)(2,1)S(1)} collective-permute-done((bf16[512,768]{1,0:T(8,128)(2,1)}, bf16[512,768]{1,0:T(8,128)(2,1)S(1)}, u32[]{:S(2)}, u32[]{:S(2)}) %collective-permute-start.18) | collective-permute-done | bytes 786464 | tf_op jit(solution)/shard_map/ppermute | solution.py:56
  86.2 70.5 %attend_forward.2 = (f32[544,768]{1,0:T(8,128)}, f32[544,128]{1,0:T(8,128)}, bf16[4096,768]{1,0:T(8,128)(2,1)}, bf16[4096,768]{1,0:T(8,128)(2,1)}, bf16[4096,768]{1,0:T(8,128)(2,1)}) custom-call(s32[16]{0:T(128)} %get-tuple-element.510.meta, bf16[512,768]{1,0:T(8,128)(2,1)} %copy-done.17, bf16[512,768]{1,0:T(8,128)(2,1)} %collective-permute-done.15.refs_1_, ...), custom_call_target="tpu_custom_call" | custom-call | flops 40000000000 | bytes 30000000 | tf_op jit(solution)/shard_map/attend_forward/pallas_call | solution.py:293
  156.7 29.8 %middle.2 = (bf16[512,768]{1,0:T(8,128)(2,1)}, bf16[32,768]{1,0:T(8,128)(2,1)}, bf16[560,768]{1,0:T(8,128)(2,1)}, bf16[32,768]{1,0:T(8,128)(2,1)}, f32[24,128]{1...) custom-call(s32[16]{0:T(128)} %get-tuple-element.510.meta, ...), custom_call_target="tpu_custom_call" | custom-call | flops 12000000000 | bytes 40000000 | tf_op jit(solution)/shard_map/middle/pallas_call | solution.py:640
  186.6 80.9 %attend_forward.3 = (f32[544,768]{1,0:T(8,128)}, f32[544,128]{1,0:T(8,128)}, bf16[4096,768]{1,0:T(8,128)(2,1)}, bf16[4096,768]{1,0:T(8,128)(2,1)}, bf16[4096,768]{1,0:T(8,128)(2,1)}) custom-call(s32[16]{0:T(128)S(1)} %get-tuple-element.838.meta, bf16[16,512,768]{2,1,0:T(8,128)(2,1)} %bitcast.86, bf16[4,32,768]{2,1,0:T(8,128)(2,1)} %get-tuple-element.647.refs_1_.memory, ...), custom_call_target="tpu_custom_call" | custom-call | flops 40000000000 | bytes 30000000 | tf_op jit(solution)/shard_map/attend_forward/pallas_call | solution.py:293
  267.6 29.6 %middle.3 = (bf16[512,768]{1,0:T(8,128)(2,1)}, bf16[32,768]{1,0:T(8,128)(2,1)}, bf16[560,768]{1,0:T(8,128)(2,1)}, bf16[32,768]{1,0:T(8,128)(2,1)S(1)}, f32[24,12...) custom-call(s32[16]{0:T(128)S(1)} %get-tuple-element.838.meta, ...), custom_call_target="tpu_custom_call" | custom-call | flops 12000000000 | bytes 40000000 | tf_op jit(solution)/shard_map/middle/pallas_call | solution.py:640
  302.7 4.1 fusion.39
  306.8 8.0 %fusion.23 = bf16[768,3072]{1,0:T(8,128)(2,1)} fusion(bf16[544,3072]{1,0:T(8,128)(2,1)S(1)} %copy-done.44, bf16[544,3072]{1,0:T(8,128)(2,1)S(1)} %copy-done.43, bf16[544,768]{1,0:T(8,128)(2,1)S(1)} %copy-done.49, bf16[544,768]{1,0:T(8,128)(2,1)S(1)} %copy-done.48), kind=kOutput, calls=%fused_computation.45 | convolution fusion | flops 5152899072 | bytes 13074432 | tf_op jit(solution)/shard_map/dot_general | solution.py:755
  314.9 8.2 %fusion.20 = bf16[3072,768]{1,0:T(8,128)(2,1)} fusion(bf16[544,3072]{1,0:T(8,128)(2,1)S(1)} %copy-done.51, bf16[544,3072]{1,0:T(8,128)(2,1)S(1)} %copy-done.50, bf16[544,768]{1,0:T(8,128)(2,1)S(1)} %copy-done.53, bf16[544,768]{1,0:T(8,128)(2,1)S(1)} %copy-done.52), kind=kOutput, calls=%fused_computation.44 | convolution fusion | flops 5152899072 | bytes 13074432 | tf_op jit(solution)/shard_map/dot_general | solution.py:755
  325.7 94.3 %attend_backward.6 = (bf16[544,768]{1,0:T(8,128)(2,1)}, bf16[544,768]{1,0:T(8,128)(2,1)}, bf16[544,768]{1,0:T(8,128)(2,1)}) custom-call(s32[16]{0:T(128)} %get-tuple-element.510.meta, bf16[16,560,768]{2,1,0:T(8,128)(2,1)} %bitcast.85, bf16[4096,768]{1,0:T(8,128)(2,1)} %get-tuple-element.512.refs_1_, bf16[4096,768]{1,0:T(8,128)(2,1)} %get-tuple-element.513.refs_2_, ...), custom_call_target="tpu_custom_call" | custom-call | flops 10000000000 | bytes 1000000 | tf_op jit(solution)/shard_map/attend_backward/pallas_call | solution.py:434
  423.6 293.3 %while.15 = (s32[]{:T(128)}, bf16[2816,768]{1,0:T(8,128)(2,1)}, bf16[2,512,768]{2,1,0:T(8,128)(2,1)}, s32[]{:T(128)}, s32[]{:T(128)}, /*index=5*/s32[16]{0:T(128...) while((s32[]{:T(128)}, bf16[2816,768]{1,0:T(8,128)(2,1)}, ...), condition=%wide.region_1.2_spmd, body=%wide.region_0.1_spmd.sunk | while | flops 13634839552 | bytes 181333648 | solution.py:906
  441.1 106.3 %attend_backward.7 = (bf16[544,768]{1,0:T(8,128)(2,1)}, bf16[544,768]{1,0:T(8,128)(2,1)}, bf16[544,768]{1,0:T(8,128)(2,1)}) custom-call(s32[16]{0:T(128)} %broadcast_add_fusion.2.meta, bf16[16,560,768]{2,1,0:T(8,128)(2,1)} %get-tuple-element.921.refs_0_, bf16[4096,768]{1,0:T(8,128)(2,1)} %get-tuple-element.922.refs_1_, ...), custom_call_target="tpu_custom_call" | custom-call | flops 10000000000 | bytes 1000000 | tf_op jit(solution)/shard_map/while/body/attend_backward/pallas_call | solution.py:434
  547.5 13.8 %late_sums.5 = bf16[2816,768]{1,0:T(8,128)(2,1)} custom-call(s32[2,16]{1,0:T(2,128)S(1)} %get-tuple-element.931.metas, s32[1]{0:T(128)} %bitcast.68.group, bf16[544,768]{1,0:T(8,128)(2,1)} %get-tuple-element.932.refs_0_, bf16[544,768]{1,0:T(8,128)(2,1)} %get-tuple-element.933.refs_1_, f32[544,768]{1,0:T(8,128)S(1)} %get-tuple-element.934.refs_2_, ...), custom_call_target="tpu_custom_call" | custom-call | tf_op jit(solution)/shard_map/while/body/late_sums/pallas_call | solution.py:743
  575.3 27.4 %collective-permute-start.1 = (bf16[352,768]{1,0:T(8,128)(2,1)S(1)}, bf16[352,768]{1,0:T(8,128)(2,1)S(1)}, u32[]{:S(2)}, u32[]{:S(2)}) collective-permute-start(bf16[352,768]{1,0:T(8,128)(2,1)S(1)} %get-tuple-element.823), channel_id=1, source_target_pairs={{0,18},{1,19},{2,16},{3,17},{4,22},{5,23},{6,20},{7,21},{8,26},{9,... | collective-permute-start | bytes 1622024 | tf_op jit(solution)/shard_map/while/body/ppermute | solution.py:760
  605.5 15.0 %collective-permute-done.1 = bf16[352,768]{1,0:T(8,128)(2,1)S(1)} collective-permute-done((bf16[352,768]{1,0:T(8,128)(2,1)S(1)}, bf16[352,768]{1,0:T(8,128)(2,1)S(1)}, u32[]{:S(2)}, u32[]{:S(2)}) %collective-permute-start.1) | collective-permute-done | bytes 540704 | tf_op jit(solution)/shard_map/while/body/ppermute | solution.py:760
  620.5 10.5 %collective-permute-done.2 = bf16[352,768]{1,0:T(8,128)(2,1)S(1)} collective-permute-done((bf16[352,768]{1,0:T(8,128)(2,1)S(1)}, bf16[352,768]{1,0:T(8,128)(2,1)S(1)}, u32[]{:S(2)}, u32[]{:S(2)}) %collective-permute-start.2) | collective-permute-done | bytes 540704 | tf_op jit(solution)/shard_map/while/body/ppermute | solution.py:760
  635.9 3.9 collective-permute-done.4
  639.9 12.0 %collective-permute-done.5 = bf16[88,768]{1,0:T(8,128)(2,1)S(1)} collective-permute-done((bf16[88,768]{1,0:T(8,128)(2,1)S(1)}, bf16[88,768]{1,0:T(8,128)(2,1)S(1)}, u32[]{:S(2)}, u32[]{:S(2)}) %collective-permute-start.5) | collective-permute-done | bytes 135200 | tf_op jit(solution)/shard_map/while/body/ppermute | solution.py:760
  652.8 3.7 collective-permute-start.9
  656.5 5.6 collective-permute-done.7
  665.7 5.4 collective-permute-done.9
  674.9 11.8 %collective-permute-done.10 = bf16[352,768]{1,0:T(8,128)(2,1)S(1)} collective-permute-done((bf16[352,768]{1,0:T(8,128)(2,1)S(1)}, bf16[352,768]{1,0:T(8,128)(2,1)S(1)}, u32[]{:S(2)}, u32[]{:S(2)}) %collective-permute-start.10) | collective-permute-done | bytes 540704 | tf_op jit(solution)/shard_map/while/body/ppermute | solution.py:760
  686.8 3.7 collective-permute-done.11
  690.6 17.7 %collective-permute-done.12 = bf16[352,768]{1,0:T(8,128)(2,1)S(1)} collective-permute-done((bf16[352,768]{1,0:T(8,128)(2,1)S(1)}, bf16[352,768]{1,0:T(8,128)(2,1)S(1)}, u32[]{:S(2)}, u32[]{:S(2)}) %collective-permute-start.12) | collective-permute-done | bytes 540704 | tf_op jit(solution)/shard_map/while/body/ppermute | solution.py:760
  708.9 3.8 collective-permute-done.13
  718.7 5.3 slice_convert_fusion
  727.0 5.0 convert_element_type.204
  732.1 4.5 convert_element_type.207
  (246 shorter events, 80.4 us)
Async XLA Ops:
  7.2 179.4 %all-gather.7.cloned.1.call-start = ((), (), s32[]{:S(2)}) async-start(), calls=%async_computation | async-start | bytes 13369344 | tf_op jit(solution)/shard_map/all_gather | solution.py:70
  9.7 21.8 %collective-permute-start.14 = (bf16[512,768]{1,0:T(8,128)(2,1)S(1)}, bf16[512,768]{1,0:T(8,128)(2,1)S(1)}, u32[]{:S(2)}, u32[]{:S(2)}) collective-permute-start(bf16[512,768]{1,0:T(8,128)(2,1)S(1)} %get-tuple-element.468.refs_0_.tokens), channel_id=1, source_target_pairs={{0,4},{1,5},{2,6},{3,7},{4,8},{5,9},{6,10},{7,11},{8,12},{9,13},{1... | collective-permute-start | bytes 2359304 | tf_op jit(solution)/shard_map/ppermute | solution.py:56
  14.8 20.9 %collective-permute-start.16 = (bf16[512,768]{1,0:T(8,128)(2,1)S(1)}, bf16[512,768]{1,0:T(8,128)(2,1)S(1)}, u32[]{:S(2)}, u32[]{:S(2)}) collective-permute-start(bf16[512,768]{1,0:T(8,128)(2,1)S(1)} %get-tuple-element.468.refs_0_.tokens), channel_id=1, source_target_pairs={{4,0},{5,1},{6,2},{7,3},{8,4},{9,5},{10,6},{11,7},{12,8},{13,9},{1... | collective-permute-start | bytes 2359304 | tf_op jit(solution)/shard_map/ppermute | solution.py:56
  16.1 21.6 %collective-permute-start.15 = (bf16[512,768]{1,0:T(8,128)(2,1)S(1)}, bf16[512,768]{1,0:T(8,128)(2,1)}, u32[]{:S(2)}, u32[]{:S(2)}) collective-permute-start(bf16[512,768]{1,0:T(8,128)(2,1)S(1)} %get-tuple-element.468.refs_0_.tokens), channel_id=1, source_target_pairs={{0,2},{1,3},{2,0},{3,1},{4,6},{5,7},{6,4},{7,5},{8,10},{9,11},{10,... | collective-permute-start | bytes 2359304 | tf_op jit(solution)/shard_map/ppermute | solution.py:56
  35.8 22.4 %collective-permute-start.19 = (bf16[512,768]{1,0:T(8,128)(2,1)S(1)}, bf16[512,768]{1,0:T(8,128)(2,1)S(1)}, u32[]{:S(2)}, u32[]{:S(2)}) collective-permute-start(bf16[512,768]{1,0:T(8,128)(2,1)S(1)} %broadcast_select_fusion), channel_id=1, source_target_pairs={{2,6},{3,7},{4,0},{5,1},{6,10},{7,11},{8,4},{9,5},{10,14},{11,15},... | collective-permute-start | bytes 2359304 | tf_op jit(solution)/shard_map/ppermute | solution.py:56
  37.1 21.6 %collective-permute-start.21 = (bf16[512,768]{1,0:T(8,128)(2,1)S(1)}, bf16[512,768]{1,0:T(8,128)(2,1)S(1)}, u32[]{:S(2)}, u32[]{:S(2)}) collective-permute-start(bf16[512,768]{1,0:T(8,128)(2,1)S(1)} %get-tuple-element.468.refs_0_.tokens), channel_id=1, source_target_pairs={{0,1},{1,0},{2,3},{3,2},{4,5},{5,4},{6,7},{7,6},{8,9},{9,8},{10,11... | collective-permute-start | bytes 2359304 | tf_op jit(solution)/shard_map/ppermute | solution.py:56
  37.2 21.6 %collective-permute-start.23 = (bf16[512,768]{1,0:T(8,128)(2,1)S(1)}, bf16[512,768]{1,0:T(8,128)(2,1)S(1)}, u32[]{:S(2)}, u32[]{:S(2)}) collective-permute-start(bf16[512,768]{1,0:T(8,128)(2,1)S(1)} %collective-permute-done.14.refs_2_), channel_id=1, source_target_pairs={{0,1},{1,0},{2,3},{3,2},{4,5},{5,4},{6,7},{7,6},{8,9},{9,8},{10,11... | collective-permute-start | bytes 2359304 | tf_op jit(solution)/shard_map/ppermute | solution.py:56
  37.7 21.9 %collective-permute-start.17 = (bf16[512,768]{1,0:T(8,128)(2,1)}, bf16[512,768]{1,0:T(8,128)(2,1)S(1)}, u32[]{:S(2)}, u32[]{:S(2)}) collective-permute-start(bf16[512,768]{1,0:T(8,128)(2,1)} %collective-permute-done.15.refs_1_), channel_id=1, source_target_pairs={{0,4},{1,5},{2,6},{3,7},{4,8},{5,9},{6,10},{7,11},{8,12},{9,13},{1... | collective-permute-start | bytes 2359304 | tf_op jit(solution)/shard_map/ppermute | solution.py:56
  42.3 30.5 %collective-permute-start.18 = (bf16[512,768]{1,0:T(8,128)(2,1)}, bf16[512,768]{1,0:T(8,128)(2,1)S(1)}, u32[]{:S(2)}, u32[]{:S(2)}) collective-permute-start(bf16[512,768]{1,0:T(8,128)(2,1)} %collective-permute-done.15.refs_1_), channel_id=1, source_target_pairs={{4,0},{5,1},{6,2},{7,3},{8,4},{9,5},{10,6},{11,7},{12,8},{13,9},{1... | collective-permute-start | bytes 2359304 | tf_op jit(solution)/shard_map/ppermute | solution.py:56
  58.2 15.0 %collective-permute-start.20 = (bf16[512,768]{1,0:T(8,128)(2,1)S(1)}, bf16[512,768]{1,0:T(8,128)(2,1)S(1)}, u32[]{:S(2)}, u32[]{:S(2)}) collective-permute-start(bf16[512,768]{1,0:T(8,128)(2,1)S(1)} %collective-permute-done.19), channel_id=1, source_target_pairs={{0,2},{1,3},{2,0},{3,1},{4,6},{5,7},{6,4},{7,5},{8,10},{9,11},{10,... | collective-permute-start | bytes 2359304 | tf_op jit(solution)/shard_map/ppermute | solution.py:56
  58.7 14.5 %collective-permute-start.22 = (bf16[512,768]{1,0:T(8,128)(2,1)}, bf16[512,768]{1,0:T(8,128)(2,1)S(1)}, u32[]{:S(2)}, u32[]{:S(2)}) collective-permute-start(bf16[512,768]{1,0:T(8,128)(2,1)} %collective-permute-done.15.refs_1_), channel_id=1, source_target_pairs={{0,1},{1,0},{2,3},{3,2},{4,5},{5,4},{6,7},{7,6},{8,9},{9,8},{10,11... | collective-permute-start | bytes 2359304 | tf_op jit(solution)/shard_map/ppermute | solution.py:56
  58.7 14.5 %collective-permute-start.24 = (bf16[512,768]{1,0:T(8,128)(2,1)S(1)}, bf16[512,768]{1,0:T(8,128)(2,1)S(1)}, u32[]{:S(2)}, u32[]{:S(2)}) collective-permute-start(bf16[512,768]{1,0:T(8,128)(2,1)S(1)} %collective-permute-done.16.refs_3_), channel_id=1, source_target_pairs={{0,1},{1,0},{2,3},{3,2},{4,5},{5,4},{6,7},{7,6},{8,9},{9,8},{10,11... | collective-permute-start | bytes 2359304 | tf_op jit(solution)/shard_map/ppermute | solution.py:56
  59.5 13.7 %collective-permute-start.25 = (bf16[512,768]{1,0:T(8,128)(2,1)S(1)}, bf16[512,768]{1,0:T(8,128)(2,1)S(1)}, u32[]{:S(2)}, u32[]{:S(2)}) collective-permute-start(bf16[512,768]{1,0:T(8,128)(2,1)S(1)} %collective-permute-done.17.refs_4_), channel_id=1, source_target_pairs={{0,1},{1,0},{2,3},{3,2},{4,5},{5,4},{6,7},{7,6},{8,9},{9,8},{10,11... | collective-permute-start | bytes 2359304 | tf_op jit(solution)/shard_map/ppermute | solution.py:56
  72.7 2.3 collective-permute-start.26
  73.2 3.1 collective-permute-start.27
  76.3 249.4 %all-gather.9.cloned.1.call-start = ((), (), s32[]{:S(2)}) async-start(), calls=%async_computation.1 | async-start | bytes 14622720 | tf_op jit(solution)/shard_map/all_gather | solution.py:70
  186.5 233.5 %all-gather.11.cloned.1.call-start = ((), (), s32[]{:S(2)}) async-start(), calls=%async_computation.2 | async-start | bytes 14622720 | tf_op jit(solution)/shard_map/all_gather | solution.py:70
  297.2 421.5 %all-reduce.5.cloned.1.call-start = ((), (), s32[]{:S(2)}) async-start(), calls=%async_computation.3 | async-start | bytes 22855680 | tf_op jit(solution)/shard_map/psum | solution.py:883
  564.3 8.6 %collective-permute-start = (bf16[1408,768]{1,0:T(8,128)(2,1)}, bf16[1408,768]{1,0:T(8,128)(2,1)}, u32[]{:S(2)}, u32[]{:S(2)}) collective-permute-start(bf16[1408,768]{1,0:T(8,128)(2,1)} %constant_dynamic-slice_fusion.11), channel_id=1, source_target_pairs={{0,1},{1,0},{2,3},{3,2},{4,5},{5,4},{6,7},{7,6},{8,9},{9,8},{10,11... | collective-permute-start | bytes 6488072 | tf_op jit(solution)/shard_map/while/body/ppermute | solution.py:760
  575.3 45.2 %collective-permute-start.1 = (bf16[352,768]{1,0:T(8,128)(2,1)S(1)}, bf16[352,768]{1,0:T(8,128)(2,1)S(1)}, u32[]{:S(2)}, u32[]{:S(2)}) collective-permute-start(bf16[352,768]{1,0:T(8,128)(2,1)S(1)} %get-tuple-element.823), channel_id=1, source_target_pairs={{0,18},{1,19},{2,16},{3,17},{4,22},{5,23},{6,20},{7,21},{8,26},{9,... | collective-permute-start | bytes 1622024 | tf_op jit(solution)/shard_map/while/body/ppermute | solution.py:760
  602.7 28.3 %collective-permute-start.2 = (bf16[352,768]{1,0:T(8,128)(2,1)S(1)}, bf16[352,768]{1,0:T(8,128)(2,1)S(1)}, u32[]{:S(2)}, u32[]{:S(2)}) collective-permute-start(bf16[352,768]{1,0:T(8,128)(2,1)S(1)} %get-tuple-element.825), channel_id=1, source_target_pairs={{0,16},{1,17},{2,18},{3,19},{4,20},{5,21},{6,22},{7,23},{8,24},{9,... | collective-permute-start | bytes 1622024 | tf_op jit(solution)/shard_map/while/body/ppermute | solution.py:760
  602.7 28.4 %collective-permute-start.3 = (bf16[352,768]{1,0:T(8,128)(2,1)S(1)}, bf16[352,768]{1,0:T(8,128)(2,1)S(1)}, u32[]{:S(2)}, u32[]{:S(2)}) collective-permute-start(bf16[352,768]{1,0:T(8,128)(2,1)S(1)} %get-tuple-element.826), channel_id=1, source_target_pairs={{0,2},{1,3},{2,0},{3,1},{4,6},{5,7},{6,4},{7,5},{8,10},{9,11},{10,... | collective-permute-start | bytes 1622024 | tf_op jit(solution)/shard_map/while/body/ppermute | solution.py:760
  631.5 8.4 %collective-permute-start.4 = (bf16[88,768]{1,0:T(8,128)(2,1)S(1)}, bf16[88,768]{1,0:T(8,128)(2,1)S(1)}, u32[]{:S(2)}, u32[]{:S(2)}) collective-permute-start(bf16[88,768]{1,0:T(8,128)(2,1)S(1)} %get-tuple-element.827), channel_id=1, source_target_pairs={{0,12},{1,13},{2,14},{3,15},{4,8},{5,9},{6,10},{7,11},{8,4},{9,5},... | collective-permute-start | bytes 405512 | tf_op jit(solution)/shard_map/while/body/ppermute | solution.py:760
  631.6 20.3 %collective-permute-start.5 = (bf16[88,768]{1,0:T(8,128)(2,1)S(1)}, bf16[88,768]{1,0:T(8,128)(2,1)S(1)}, u32[]{:S(2)}, u32[]{:S(2)}) collective-permute-start(bf16[88,768]{1,0:T(8,128)(2,1)S(1)} %get-tuple-element.828), channel_id=1, source_target_pairs={{0,8},{1,9},{2,10},{3,11},{4,12},{5,13},{6,14},{7,15},{8,0},{9,1},... | collective-permute-start | bytes 405512 | tf_op jit(solution)/shard_map/while/body/ppermute | solution.py:760
  634.5 17.4 %collective-permute-start.6 = (bf16[88,768]{1,0:T(8,128)(2,1)S(1)}, bf16[88,768]{1,0:T(8,128)(2,1)S(1)}, u32[]{:S(2)}, u32[]{:S(2)}) collective-permute-start(bf16[88,768]{1,0:T(8,128)(2,1)S(1)} %get-tuple-element.829), channel_id=1, source_target_pairs={{0,4},{1,5},{2,6},{3,7},{4,0},{5,1},{6,2},{7,3},{8,12},{9,13},{10,... | collective-permute-start | bytes 405512 | tf_op jit(solution)/shard_map/while/body/ppermute | solution.py:760
  652.0 10.1 %collective-permute-start.7 = (bf16[88,768]{1,0:T(8,128)(2,1)S(1)}, bf16[88,768]{1,0:T(8,128)(2,1)S(1)}, u32[]{:S(2)}, u32[]{:S(2)}) collective-permute-start(bf16[88,768]{1,0:T(8,128)(2,1)S(1)} %get-tuple-element.831), channel_id=1, source_target_pairs={{0,4},{1,5},{2,6},{3,7},{4,0},{5,1},{6,2},{7,3},{8,12},{9,13},{10,... | collective-permute-start | bytes 405512 | tf_op jit(solution)/shard_map/while/body/ppermute | solution.py:760
  652.1 13.6 %collective-permute-start.8 = (bf16[88,768]{1,0:T(8,128)(2,1)S(1)}, bf16[88,768]{1,0:T(8,128)(2,1)S(1)}, u32[]{:S(2)}, u32[]{:S(2)}) collective-permute-start(bf16[88,768]{1,0:T(8,128)(2,1)S(1)} %get-tuple-element.831), channel_id=1, source_target_pairs={{0,8},{1,9},{2,10},{3,11},{4,12},{5,13},{6,14},{7,15},{8,0},{9,1},... | collective-permute-start | bytes 405512 | tf_op jit(solution)/shard_map/while/body/ppermute | solution.py:760
  652.8 18.3 %collective-permute-start.9 = (bf16[88,768]{1,0:T(8,128)(2,1)S(1)}, bf16[88,768]{1,0:T(8,128)(2,1)S(1)}, u32[]{:S(2)}, u32[]{:S(2)}) collective-permute-start(bf16[88,768]{1,0:T(8,128)(2,1)S(1)} %get-tuple-element.831), channel_id=1, source_target_pairs={{0,12},{1,13},{2,14},{3,15},{4,8},{5,9},{6,10},{7,11},{8,4},{9,5},... | collective-permute-start | bytes 405512 | tf_op jit(solution)/shard_map/while/body/ppermute | solution.py:760
  671.2 15.6 %collective-permute-start.10 = (bf16[352,768]{1,0:T(8,128)(2,1)S(1)}, bf16[352,768]{1,0:T(8,128)(2,1)S(1)}, u32[]{:S(2)}, u32[]{:S(2)}) collective-permute-start(bf16[352,768]{1,0:T(8,128)(2,1)S(1)} %constant_dynamic-update-slice_fusion.23), channel_id=1, source_target_pairs={{0,2},{1,3},{2,0},{3,1},{4,6},{5,7},{6,4},{7,5},{8,10},{9,11},{10,... | collective-permute-start | bytes 1622024 | tf_op jit(solution)/shard_map/while/body/ppermute | solution.py:760
  672.8 17.7 %collective-permute-start.11 = (bf16[352,768]{1,0:T(8,128)(2,1)S(1)}, bf16[352,768]{1,0:T(8,128)(2,1)S(1)}, u32[]{:S(2)}, u32[]{:S(2)}) collective-permute-start(bf16[352,768]{1,0:T(8,128)(2,1)S(1)} %constant_dynamic-update-slice_fusion.23), channel_id=1, source_target_pairs={{0,16},{1,17},{2,18},{3,19},{4,20},{5,21},{6,22},{7,23},{8,24},{9,... | collective-permute-start | bytes 1622024 | tf_op jit(solution)/shard_map/while/body/ppermute | solution.py:760
  672.8 35.4 %collective-permute-start.12 = (bf16[352,768]{1,0:T(8,128)(2,1)S(1)}, bf16[352,768]{1,0:T(8,128)(2,1)S(1)}, u32[]{:S(2)}, u32[]{:S(2)}) collective-permute-start(bf16[352,768]{1,0:T(8,128)(2,1)S(1)} %constant_dynamic-update-slice_fusion.23), channel_id=1, source_target_pairs={{0,18},{1,19},{2,16},{3,17},{4,22},{5,23},{6,20},{7,21},{8,26},{9,... | collective-permute-start | bytes 1622024 | tf_op jit(solution)/shard_map/while/body/ppermute | solution.py:760
  708.3 4.5 collective-permute-start.13
  (60 other events, 1517.6 us)
Sparse Core Ops, SparseCore 0:
  76.4 102.8 all-gather.6
  186.6 119.2 all-gather.8
  308.8 107.5 all-gather.10
  423.3 295.3 all-reduce.4
